TPU v7x, 256 devices: a whole 4x4x8 slice. The times are simulated.
256 devices in a mesh: row: 32 (over z_hi, x, y), col: 8 (over z_lo, core).
Axes of the slice: x: 4, y: 4, z: 8 (z_hi: 2, z_lo: 4; z = z_hi * 4 + z_lo), core: 2. Of those that a mesh axis runs over, the one named last changes fastest.
Arguments:
- covariance: float32 [16384, 16384], P('row', 'col'), may hold values from -1.2 to 7.2, as said below
- classes: int32 [8192], replicated, may hold values from 0 to 15
- feed_rate: float32 [16], replicated, may hold values from 0.7 to 2
- conversion_rate: float32 [16], replicated, may hold values from 0.5 to 3
- diffusion: float32 [2], replicated, may hold values from 0.3 to 2
Outputs:
- advanced: float32 [16384, 16384], P('row', 'col')
Inputs may be any that keep to these rules, and one draw needn't show every extreme that they name: covariance is symmetric: entry (r, c) equals entry (c, r) exactly.
All inputs are finite; a program needn't handle non-finite values.
Results may differ from a plain program's by a relative error of at most 0.00002.
Values sent between devices are 32-bit elements; how exact they have to be, the bound alone decides.
A program may use at most 128 MiB of HBM per device.

v0:
```python
import jax
import jax.numpy as jnp
from jax import lax
from jax.sharding import PartitionSpec as P

VOXELS = 8192


step_size = 0.04


def extended(value, sides, width):
    for axis, dim in sides:
        devices, length = (lax.axis_size(axis), value.shape[dim])
        up = [(i, (i + 1) % devices) for i in range(devices - 1)]
        down = [(j, i) for i, j in up]
        last = lax.slice_in_dim(value, length - width, length, axis=dim)
        initial = lax.slice_in_dim(value, 0, width, axis=dim)
        before = lax.ppermute(last, axis, up)
        after = lax.ppermute(initial, axis, down)
        value = jnp.concatenate([before, value, after], axis=dim)
    return value


def lookup(row_class, rate_table):
    class_ids = jnp.arange(rate_table.shape[0], dtype=jnp.int32)
    return jnp.sum(
        jnp.where(row_class[:, None] == class_ids[None, :], rate_table[None, :], 0.0), axis=1
    )


def coefficients(row_class, positions, feed_rate, conversion_rate, diffusion, voxels):
    feed_here = lookup(row_class, feed_rate)
    conv_here = lookup(row_class, conversion_rate)
    voxel_ids = positions // 2
    is_even = positions % 2 == 0
    neighbours = (
        2.0
        - (voxel_ids == 0).astype(feed_here.dtype)
        - (voxel_ids == voxels - 1).astype(feed_here.dtype)
    )
    diff_coef = jnp.where(is_even, diffusion[0], diffusion[1])
    square_feed = feed_here * feed_here
    self_coef = jnp.where(is_even, conv_here - 1.0, -square_feed) - diff_coef * neighbours
    cross_coef = jnp.where(is_even, square_feed, -conv_here)
    product_rate = feed_here * conv_here
    noise_same = jnp.where(is_even, 2.0 * feed_here + 2.0 * product_rate, 2.0 * product_rate)
    noise_cross = -2.0 * product_rate
    return (self_coef, cross_coef, diff_coef, noise_same, noise_cross)


def local_rates(classes, feed_rate, conversion_rate, diffusion, first_index, amount):
    voxel_class = lax.dynamic_slice_in_dim(classes, first_index // 2, amount // 2)
    row_class = jnp.repeat(voxel_class, 2, total_repeat_length=amount)
    positions = first_index + jnp.arange(amount, dtype=jnp.int32)
    return (
        positions,
        coefficients(row_class, positions, feed_rate, conversion_rate, diffusion, VOXELS),
    )


def stencil_rows(padded, self_coef, cross_coef, diff_coef, is_even):
    centre = padded[2:-2]
    partner = jnp.where(is_even[:, None], padded[3:-1], padded[1:-3])
    return (
        self_coef[:, None] * centre
        + cross_coef[:, None] * partner
        + diff_coef[:, None] * (padded[:-4] + padded[4:])
    )


def stencil_cols(padded, self_coef, cross_coef, diff_coef, is_even):
    centre = padded[:, 2:-2]
    partner = jnp.where(is_even[None, :], padded[:, 3:-1], padded[:, 1:-3])
    return (
        self_coef[None, :] * centre
        + cross_coef[None, :] * partner
        + diff_coef[None, :] * (padded[:, :-4] + padded[:, 4:])
    )


def body(covariance, classes, feed_rate, conversion_rate, diffusion):
    tile_rows, tile_cols = covariance.shape
    row_first = lax.axis_index("row") * tile_rows
    col_first = lax.axis_index("col") * tile_cols
    row_positions, row_coefs = local_rates(
        classes, feed_rate, conversion_rate, diffusion, row_first, tile_rows
    )
    self_coef, cross_coef, diff_coef, noise_same, noise_cross = row_coefs
    row_even = row_positions % 2 == 0
    col_positions = col_first + jnp.arange(tile_cols, dtype=jnp.int32)
    same_voxel = (row_positions // 2)[:, None] == (col_positions // 2)[None, :]
    same_parity = (row_positions % 2)[:, None] == (col_positions % 2)[None, :]
    noise_tile = jnp.where(
        same_voxel, jnp.where(same_parity, noise_same[:, None], noise_cross[:, None]), 0.0
    )

    def rate_of(field):
        col_coefs = local_rates(
            classes, feed_rate, conversion_rate, diffusion, col_first, tile_cols
        )[1]
        col_even = col_positions % 2 == 0
        padded = extended(field, (("row", 0), ("col", 1)), 2)
        forward = stencil_rows(padded[:, 2:-2], self_coef, cross_coef, diff_coef, row_even)
        backward = stencil_cols(padded[2:-2, :], col_coefs[0], col_coefs[1], col_coefs[2], col_even)
        return forward + backward + noise_tile

    first_rate = rate_of(covariance)
    section_cov = covariance + step_size * first_rate
    second_rate = rate_of(section_cov)
    return covariance + 0.5 * step_size * (first_rate + second_rate)


def solution(mesh):
    in_specs = (P("row", "col"), P(), P(), P(), P())
    out_specs = P("row", "col")
    return jax.shard_map(body, mesh=mesh, in_specs=in_specs, out_specs=out_specs, check_vma=False)
```

profile of v0, /device:TPU:129, one launch (start us, length us, event | category | flops | bytes accessed | tf_op | source)
XLA Modules:
  0.0 107.0 jit_solution(13602742259890402350)
XLA Ops:
  0.9 3.2 %collective-permute-start.1 = (f32[2,2048]{1,0:T(2,128)S(1)}, f32[2,2048]{1,0:T(2,128)S(1)}, u32[]{:S(2)}, u32[]{:S(2)}) collective-permute-start(f32[2,2048]{1,0:T(2,128)S(1)} %get-tuple-element.54), channel_id=1, source_target_pairs={{0,8},{8,16},{16,24},{24,32},{32,40},{40,48},{48,56},{56,64},{64,7... | collective-permute-start | bytes 49160 | tf_op jit(solution)/shard_map/ppermute | solution.py:19
  4.1 10.2 %collective-permute-start = (f32[2,2048]{1,0:T(2,128)S(1)}, f32[2,2048]{1,0:T(2,128)S(1)}, u32[]{:S(2)}, u32[]{:S(2)}) collective-permute-start(f32[2,2048]{1,0:T(2,128)S(1)} %get-tuple-element.55), channel_id=1, source_target_pairs={{8,0},{16,8},{24,16},{32,24},{40,32},{48,40},{56,48},{64,56},{72,6... | collective-permute-start | bytes 49160 | tf_op jit(solution)/shard_map/ppermute | solution.py:20
  14.4 1.4 %fusion.42 = (f32[1]{0:T(128)}, f32[1]{0:T(128)}) fusion(f32[2]{0:T(128)} %param.17), kind=kLoop, calls=%fused_computation.113 | loop fusion | bytes 16 | tf_op jit(solution)/shard_map/slice | solution.py:42
  15.8 1.3 %broadcast_select_fusion.1 = f32[512]{0:T(512)S(1)} fusion(f32[]{:T(128)} %bitcast.9, f32[]{:T(128)} %bitcast.8, s32[]{:T(128)S(6)} %mul.173), kind=kLoop, calls=%fused_computation.105 | loop fusion | flops 7168 | bytes 2060 | tf_op jit(solution)/shard_map/jit(_where)/select_n | solution.py:42
  17.1 1.3 %broadcast_select_fusion = f32[2048]{0:T(1024)S(1)} fusion(f32[]{:T(128)} %bitcast.9, f32[]{:T(128)} %bitcast.8, s32[]{:T(128)S(6)} %mul.182), kind=kLoop, calls=%fused_computation.85 | loop fusion | flops 28672 | bytes 8204 | tf_op jit(solution)/shard_map/jit(_where)/select_n | solution.py:42
  18.5 4.6 %constant_dynamic-update-slice_fusion.1 = f32[514,2048]{1,0:T(8,128)} fusion(f32[512,2048]{1,0:T(8,128)} %param.13), kind=kLoop, calls=%fused_computation.84 | loop fusion | bytes 8388608
  23.2 2.3 %scatter_custom_fusion = s32[512]{0:T(512)S(1)} fusion(s32[256]{0:T(256)S(1)} %bitcast.21, s32[256]{0:T(256)S(1)} %broadcast.618, s32[]{:T(128)} %constant.270.clone.1), kind=kCustom, calls=%fused_computation.106 | custom fusion | flops 256 | bytes 2052 | tf_op jit(solution)/shard_map/scatter-add | solution.py:54
  26.3 3.5 %gather_fusion = s32[512]{0:T(512)S(1)} fusion(s32[256]{0:T(256)S(1)} %dynamic_slice.7, s32[1024]{0:T(1024)S(1)} %pad_clamp_fusion), kind=kCustom, calls=%fused_computation.1 | custom fusion | bytes 6144 | tf_op jit(solution)/shard_map/jit(_take)/gather | solution.py:54
  29.9 8.6 %gather_fusion.1 = s32[2048]{0:T(1024)S(1)} fusion(s32[1024]{0:T(1024)S(1)} %dynamic_slice.8, s32[2048]{0:T(1024)S(1)} %broadcast_clamp_fusion), kind=kCustom, calls=%fused_computation.clone | custom fusion | bytes 24576 | tf_op jit(solution)/shard_map/jit(_take)/gather | solution.py:54
  38.7 1.7 %multiply_subtract_fusion.1 = (f32[512]{0:T(512)S(1)}, f32[512]{0:T(512)S(1)}, f32[512]{0:T(512)S(1)}, f32[512]{0:T(512)S(1)}) fusion(f32[512]{0:T(512)S(1)} %get-tuple-element.40, f32[512]{0:T(512)S(1)} %get-tuple-element.41, s32[]{:T(128)S(6)} %mul.173, f32[]{:T(128)} %bitcast.9, f32[]{:T(128)} %bitcast.8), kind=kLoop, calls=%fused_computation.94 | loop fusion | flops 21504 | bytes 12300 | tf_op jit(solution)/shard_map/sub | solution.py:44
  40.4 1.3 %multiply_subtract_fusion = (f32[2048]{0:T(1024)S(1)}, f32[2048]{0:T(1024)S(1)}) fusion(f32[2048]{0:T(1024)S(1)} %get-tuple-element.39, f32[2048]{0:T(1024)S(1)} %get-tuple-element.38, s32[]{:T(128)S(6)} %mul.182, f32[]{:T(128)} %bitcast.9, f32[]{:T(128)} %bitcast.8), kind=kLoop, calls=%fused_computation.71 | loop fusion | flops 73728 | bytes 32780 | tf_op jit(solution)/shard_map/sub | solution.py:44
  43.0 3.8 %collective-permute-start.3 = (f32[516,2]{1,0:T(8,128)S(1)}, f32[516,2]{1,0:T(8,128)S(1)}, u32[]{:S(2)}, u32[]{:S(2)}) collective-permute-start(f32[516,2]{1,0:T(8,128)S(1)} %get-tuple-element.50), channel_id=1, source_target_pairs={{0,1},{1,2},{2,3},{3,4},{4,5},{5,6},{6,7},{8,9},{9,10},{10,11},{11... | collective-permute-start | bytes 12392 | tf_op jit(solution)/shard_map/ppermute | solution.py:19
  46.8 1.9 %collective-permute-start.2 = (f32[516,2]{1,0:T(8,128)S(1)}, f32[516,2]{1,0:T(8,128)S(1)}, u32[]{:S(2)}, u32[]{:S(2)}) collective-permute-start(f32[516,2]{1,0:T(8,128)S(1)} %get-tuple-element.51), channel_id=1, source_target_pairs={{1,0},{2,1},{3,2},{4,3},{5,4},{6,5},{7,6},{9,8},{10,9},{11,10},{12... | collective-permute-start | bytes 12392 | tf_op jit(solution)/shard_map/ppermute | solution.py:20
  50.1 4.4 %collective-permute-done.2 = f32[516,2]{1,0:T(8,128)S(1)} collective-permute-done((f32[516,2]{1,0:T(8,128)S(1)}, f32[516,2]{1,0:T(8,128)S(1)}, u32[]{:S(2)}, u32[]{:S(2)}) %collective-permute-start.2) | collective-permute-done | bytes 4160 | tf_op jit(solution)/shard_map/ppermute | solution.py:20
  54.5 4.0 %maximum_maximum_fusion = (f32[516,2050]{1,0:T(8,128)S(1)}, f32[516,2050]{1,0:T(8,128)S(1)}) fusion(f32[2,2048]{1,0:T(2,128)S(1)} %collective-permute-done, f32[512,2048]{1,0:T(8,128)S(1)} %copy-done.1, f32[2,2048]{1,0:T(2,128)S(1)} %collective-permute-done.1, f32[516,2]{1,0:T(8,128)S(1)} %collective-permute-done.3, f32[516,2]{1,0:T(8,128)S(1)} %collective-permute-done.2), kind=kLoop, calls=%fused_computation.4 | loop fusion | flops 6346800 | bytes 12697728 | tf_op jit(solution)/shard_map/concatenate | solution.py:21
  58.5 8.3 %multiply_add_fusion = (f32[512,2048]{1,0:T(8,128)S(1)}, f32[512,2048]{1,0:T(8,128)S(1)}) fusion(f32[512,2048]{1,0:T(8,128)S(1)} %copy-done.1, f32[512]{0:T(512)S(1)} %get-tuple-element.59, f32[512]{0:T(512)S(1)} %get-tuple-element.60, s32[2048]{0:T(1024)S(1)} %get-tuple-element.69, s32[512]{0:T(512)S(1)} %get-tuple-element.67, ...), kind=kLoop, calls=%fused_computation.50 | loop fusion | flops 25165824 | bytes 37822976 | tf_op jit(solution)/shard_map/add | solution.py:109
  66.9 1.9 %collective-permute-start.4 = (f32[2,2048]{1,0:T(2,128)S(1)}, f32[2,2048]{1,0:T(2,128)S(1)}, u32[]{:S(2)}, u32[]{:S(2)}) collective-permute-start(f32[2,2048]{1,0:T(2,128)S(1)} %get-tuple-element.52), channel_id=1, source_target_pairs={{8,0},{16,8},{24,16},{32,24},{40,32},{48,40},{56,48},{64,56},{72,6... | collective-permute-start | bytes 49160 | tf_op jit(solution)/shard_map/ppermute | solution.py:20
  68.8 3.4 %collective-permute-start.5 = (f32[2,2048]{1,0:T(2,128)S(1)}, f32[2,2048]{1,0:T(2,128)S(1)}, u32[]{:S(2)}, u32[]{:S(2)}) collective-permute-start(f32[2,2048]{1,0:T(2,128)S(1)} %get-tuple-element.53), channel_id=1, source_target_pairs={{0,8},{8,16},{16,24},{24,32},{32,40},{40,48},{48,56},{56,64},{64,7... | collective-permute-start | bytes 49160 | tf_op jit(solution)/shard_map/ppermute | solution.py:19
  72.2 9.2 %collective-permute-done.5 = f32[2,2048]{1,0:T(2,128)S(1)} collective-permute-done((f32[2,2048]{1,0:T(2,128)S(1)}, f32[2,2048]{1,0:T(2,128)S(1)}, u32[]{:S(2)}, u32[]{:S(2)}) %collective-permute-start.5) | collective-permute-done | bytes 16416 | tf_op jit(solution)/shard_map/ppermute | solution.py:19
  81.5 3.0 %collective-permute-start.7 = (f32[516,2]{1,0:T(8,128)S(1)}, f32[516,2]{1,0:T(8,128)S(1)}, u32[]{:S(2)}, u32[]{:S(2)}) collective-permute-start(f32[516,2]{1,0:T(8,128)S(1)} %get-tuple-element.46), channel_id=1, source_target_pairs={{0,1},{1,2},{2,3},{3,4},{4,5},{5,6},{6,7},{8,9},{9,10},{10,11},{11... | collective-permute-start | bytes 12392 | tf_op jit(solution)/shard_map/ppermute | solution.py:19
  84.6 2.1 %collective-permute-start.6 = (f32[516,2]{1,0:T(8,128)S(1)}, f32[516,2]{1,0:T(8,128)S(1)}, u32[]{:S(2)}, u32[]{:S(2)}) collective-permute-start(f32[516,2]{1,0:T(8,128)S(1)} %get-tuple-element.47), channel_id=1, source_target_pairs={{1,0},{2,1},{3,2},{4,3},{5,4},{6,5},{7,6},{9,8},{10,9},{11,10},{12... | collective-permute-start | bytes 12392 | tf_op jit(solution)/shard_map/ppermute | solution.py:20
  87.9 4.4 %collective-permute-done.6 = f32[516,2]{1,0:T(8,128)S(1)} collective-permute-done((f32[516,2]{1,0:T(8,128)S(1)}, f32[516,2]{1,0:T(8,128)S(1)}, u32[]{:S(2)}, u32[]{:S(2)}) %collective-permute-start.6) | collective-permute-done | bytes 4160 | tf_op jit(solution)/shard_map/ppermute | solution.py:20
  92.3 4.0 %maximum_maximum_fusion.1 = (f32[516,2050]{1,0:T(8,128)S(1)}, f32[516,2050]{1,0:T(8,128)S(1)}) fusion(f32[2,2048]{1,0:T(2,128)S(1)} %collective-permute-done.4, f32[512,2048]{1,0:T(8,128)S(1)} %get-tuple-element.42, f32[2,2048]{1,0:T(2,128)S(1)} %collective-permute-done.5, f32[516,2]{1,0:T(8,128)S(1)} %collective-permute-done.7, ...), kind=kLoop, calls=%fused_computation.6 | loop fusion | flops 6346800 | bytes 12697728 | tf_op jit(solution)/shard_map/concatenate | solution.py:21
  96.3 10.6 %fusion.9 = f32[512,2048]{1,0:T(8,128)} fusion(f32[512,2048]{1,0:T(8,128)S(1)} %copy-done.1, f32[512,2048]{1,0:T(8,128)S(1)} %get-tuple-element.43, f32[2,2048]{1,0:T(2,128)S(1)} %collective-permute-done.5, f32[512,2048]{1,0:T(8,128)S(1)} %get-tuple-element.42, f32[2,2048]{1,0:T(2,128)S(1)} %collective-permute-done.4, f32[516,2050]{1,0:T(8,128)S(1)} %get-tuple-element.45, ...), kind=kLoop, calls=%fused_computation.22 | loop fusion | flops 28311552 | bytes 33645056 | tf_op jit(solution)/shard_map/add | solution.py:111
  (45 shorter events, 6.0 us)
Async XLA Ops:
  0.0 26.2 %copy-start = (s32[8192]{0:T(1024)S(1)}, s32[8192]{0:T(1024)}, u32[]{:S(2)}) copy-start(s32[8192]{0:T(1024)} %param.14) | copy-start | bytes 98308
  0.9 40.9 %collective-permute-start.1 = (f32[2,2048]{1,0:T(2,128)S(1)}, f32[2,2048]{1,0:T(2,128)S(1)}, u32[]{:S(2)}, u32[]{:S(2)}) collective-permute-start(f32[2,2048]{1,0:T(2,128)S(1)} %get-tuple-element.54), channel_id=1, source_target_pairs={{0,8},{8,16},{16,24},{24,32},{32,40},{40,48},{48,56},{56,64},{64,7... | collective-permute-start | bytes 49160 | tf_op jit(solution)/shard_map/ppermute | solution.py:19
  4.1 37.7 %collective-permute-start = (f32[2,2048]{1,0:T(2,128)S(1)}, f32[2,2048]{1,0:T(2,128)S(1)}, u32[]{:S(2)}, u32[]{:S(2)}) collective-permute-start(f32[2,2048]{1,0:T(2,128)S(1)} %get-tuple-element.55), channel_id=1, source_target_pairs={{8,0},{16,8},{24,16},{32,24},{40,32},{48,40},{56,48},{64,56},{72,6... | collective-permute-start | bytes 49160 | tf_op jit(solution)/shard_map/ppermute | solution.py:20
  18.5 4.7 %copy-start.6 = (s32[2,128]{1,0:T(2,128)S(1)}, s32[2,128]{1,0:T(2,128)}, u32[]{:S(2)}) copy-start(s32[2,128]{1,0:T(2,128)} %constant.274.clone.1) | copy-start | bytes 3076
  18.5 11.4 %copy-start.3 = (s32[2048]{0:T(1024)S(1)}, s32[2048]{0:T(1024)}, u32[]{:S(2)}) copy-start(s32[2048]{0:T(1024)} %constant.290) | copy-start | bytes 24580
  29.9 8.6 %copy-start.4 = (f32[16]{0:T(128)S(1)}, f32[16]{0:T(128)}, u32[]{:S(2)}) copy-start(f32[16]{0:T(128)} %param.16) | copy-start | bytes 196
  29.9 8.6 %copy-start.5 = (f32[16]{0:T(128)S(1)}, f32[16]{0:T(128)}, u32[]{:S(2)}) copy-start(f32[16]{0:T(128)} %param.15) | copy-start | bytes 196
  38.5 16.0 %copy-start.1 = (f32[512,2048]{1,0:T(8,128)S(1)}, f32[512,2048]{1,0:T(8,128)}, u32[]{:S(2)}) copy-start(f32[512,2048]{1,0:T(8,128)} %param.13) | copy-start | bytes 12582916
  43.0 7.1 %collective-permute-start.3 = (f32[516,2]{1,0:T(8,128)S(1)}, f32[516,2]{1,0:T(8,128)S(1)}, u32[]{:S(2)}, u32[]{:S(2)}) collective-permute-start(f32[516,2]{1,0:T(8,128)S(1)} %get-tuple-element.50), channel_id=1, source_target_pairs={{0,1},{1,2},{2,3},{3,4},{4,5},{5,6},{6,7},{8,9},{9,10},{10,11},{11... | collective-permute-start | bytes 12392 | tf_op jit(solution)/shard_map/ppermute | solution.py:19
  46.8 7.7 %collective-permute-start.2 = (f32[516,2]{1,0:T(8,128)S(1)}, f32[516,2]{1,0:T(8,128)S(1)}, u32[]{:S(2)}, u32[]{:S(2)}) collective-permute-start(f32[516,2]{1,0:T(8,128)S(1)} %get-tuple-element.51), channel_id=1, source_target_pairs={{1,0},{2,1},{3,2},{4,3},{5,4},{6,5},{7,6},{9,8},{10,9},{11,10},{12... | collective-permute-start | bytes 12392 | tf_op jit(solution)/shard_map/ppermute | solution.py:20
  49.3 9.2 %copy-start.2 = (f32[514,2048]{1,0:T(8,128)S(1)}, f32[514,2048]{1,0:T(8,128)}, u32[]{:S(2)}) copy-start(f32[514,2048]{1,0:T(8,128)} %constant_dynamic-update-slice_fusion) | copy-start | bytes 12632068
  66.9 5.3 %collective-permute-start.4 = (f32[2,2048]{1,0:T(2,128)S(1)}, f32[2,2048]{1,0:T(2,128)S(1)}, u32[]{:S(2)}, u32[]{:S(2)}) collective-permute-start(f32[2,2048]{1,0:T(2,128)S(1)} %get-tuple-element.52), channel_id=1, source_target_pairs={{8,0},{16,8},{24,16},{32,24},{40,32},{48,40},{56,48},{64,56},{72,6... | collective-permute-start | bytes 49160 | tf_op jit(solution)/shard_map/ppermute | solution.py:20
  68.8 12.6 %collective-permute-start.5 = (f32[2,2048]{1,0:T(2,128)S(1)}, f32[2,2048]{1,0:T(2,128)S(1)}, u32[]{:S(2)}, u32[]{:S(2)}) collective-permute-start(f32[2,2048]{1,0:T(2,128)S(1)} %get-tuple-element.53), channel_id=1, source_target_pairs={{0,8},{8,16},{16,24},{24,32},{32,40},{40,48},{48,56},{56,64},{64,7... | collective-permute-start | bytes 49160 | tf_op jit(solution)/shard_map/ppermute | solution.py:19
  81.5 6.4 %collective-permute-start.7 = (f32[516,2]{1,0:T(8,128)S(1)}, f32[516,2]{1,0:T(8,128)S(1)}, u32[]{:S(2)}, u32[]{:S(2)}) collective-permute-start(f32[516,2]{1,0:T(8,128)S(1)} %get-tuple-element.46), channel_id=1, source_target_pairs={{0,1},{1,2},{2,3},{3,4},{4,5},{5,6},{6,7},{8,9},{9,10},{10,11},{11... | collective-permute-start | bytes 12392 | tf_op jit(solution)/shard_map/ppermute | solution.py:19
  84.6 7.7 %collective-permute-start.6 = (f32[516,2]{1,0:T(8,128)S(1)}, f32[516,2]{1,0:T(8,128)S(1)}, u32[]{:S(2)}, u32[]{:S(2)}) collective-permute-start(f32[516,2]{1,0:T(8,128)S(1)} %get-tuple-element.47), channel_id=1, source_target_pairs={{1,0},{2,1},{3,2},{4,3},{5,4},{6,5},{7,6},{9,8},{10,9},{11,10},{12... | collective-permute-start | bytes 12392 | tf_op jit(solution)/shard_map/ppermute | solution.py:20
where the time goes:
time: 107 us
  other arithmetic  37.1 us (35%)
  starting transfers between devices  29.5 us (28%)
  waiting for transfers between devices  20.1 us (19%)
  local copies, waits for them, and re-layouts  20 us (19%)
    ppermute x4, starting transfers between devices, extended(): after = lax.ppermute(initial, axis, down)  16.1 us
    ppermute x4, starting transfers between devices, extended(): before = lax.ppermute(last, axis, up)  13.4 us
    gather x2, local copies, waits for them, and re-layouts, local_rates(): row_class = jnp.repeat(voxel_class, 2, total_repeat_length=amount)  12.1 us
    ppermute x4, waiting for transfers between devices, extended(): before = lax.ppermute(last, axis, up)  11.3 us
    add x1, other arithmetic, body(): return covariance + 0.5 * step_size * (first_rate + second_rate)  10.6 us
    concatenate x4, other arithmetic, extended(): value = jnp.concatenate([before, value, after], axis=dim)  9.37 us
    ppermute x4, waiting for transfers between devices, extended(): after = lax.ppermute(initial, axis, down)  8.8 us
    add x1, other arithmetic, body(): section_cov = covariance + step_size * first_rate  8.29 us
  transfers between devices with their start and end apart: 8, of which 5 were waited for; matrix products, arithmetic and copies ran while one was open for 26% of the time, Pallas kernels for 0%

commit v1 on v0

v1 whole, which is shorter than its diff:
```python
import functools

import jax
import jax.numpy as jnp
from jax import lax
from jax.experimental import pallas as pl
from jax.experimental.pallas import tpu as pltpu
from jax.sharding import PartitionSpec as P

STEP = 0.04
LANES = 128
PAD = 8
F32, BF16 = jnp.float32, jnp.bfloat16
MESH = pl.DeviceIdType.MESH
SIDES = [(dr, dc) for dr in (-1, 0, 1) for dc in (-1, 0, 1) if (dr, dc) != (0, 0)]


def split(value):
    high = value.astype(BF16)
    return high, (value - high.astype(F32)).astype(BF16)


def iota(shape, dim):
    return lax.broadcasted_iota(jnp.int32, shape, dim)


def advance_kernel(
    rows, panels, voxels, grid_rows, grid_cols,
    cov, classes, feed, conv, diff,
    u_ref, ge, go, full,
    vx, high, low, whi, wlo, code, half, noise, feed_of, conv_of, ext_s, ext_x, ext_a, ext_b, col,
    send_row, send_col, got_row, got_col, got_corner, tile_g,
    load_sem, edge_sem, send_sem, recv_sem,
):
    row, cols_at = lax.axis_index("row"), lax.axis_index("col")
    groups = rows // 16
    half_rows = rows // 2
    d0, d1 = diff[0] * STEP, diff[1] * STEP

    def there(dr, dc):
        ok = None
        for at, step, size in ((row, dr, grid_rows), (cols_at, dc, grid_cols)):
            if step:
                one = (at + step >= 0) & (at + step < size)
                ok = one if ok is None else ok & one
        return ok

    barrier = pltpu.get_barrier_semaphore()
    count = jnp.int32(0)
    for dr, dc in SIDES:
        ok = there(dr, dc)
        count += ok.astype(jnp.int32)

        @pl.when(ok)
        def _(dr=dr, dc=dc):
            pl.semaphore_signal(barrier, inc=1, device_id=(row + dr, cols_at + dc), device_id_type=MESH)

    def load(p):
        return pltpu.make_async_copy(
            cov.at[:, pl.ds(pl.multiple_of(p * LANES, LANES), LANES)],
            vx.at[p + 1, pl.ds(PAD, rows), :],
            load_sem.at[p],
        )

    load(0).start()
    load(panels - 1).start()

    def start_load(p, _):
        load(p).start()
        return 0

    lax.fori_loop(1, panels - 1, start_load, 0)

    zero = jnp.zeros((8, LANES), F32)
    for p in range(panels):
        vx[p + 1, 0:PAD, :] = zero
        vx[p + 1, PAD + rows : 2 * PAD + rows, :] = zero
    for i, (step, at) in enumerate(((1, 0), (-1, grid_rows - 1))):
        @pl.when(row == at)
        def _(i=i):
            got_row[i] = jnp.zeros(got_row.shape[1:], F32)
    for i, at in enumerate((0, grid_cols - 1)):
        @pl.when(cols_at == at)
        def _(i=i):
            got_col[i] = jnp.zeros(got_col.shape[1:], F32)
    for i, (dr, dc) in enumerate(((-1, -1), (-1, 1), (1, -1), (1, 1))):
        @pl.when(jnp.logical_not(there(dr, dc)))
        def _(i=i):
            got_corner[i] = zero

    ids = classes[...]
    a_all, b_all = jnp.zeros(ids.shape, F32), jnp.zeros(ids.shape, F32)
    for k in range(feed.shape[0]):
        a_all = jnp.where(ids == k, feed[k], a_all)
        b_all = jnp.where(ids == k, conv[k], b_all)
    feed_of[...] = a_all
    conv_of[...] = b_all
    class_rows = voxels // LANES

    lane8 = iota((8, LANES), 1)
    row_at = row * (half_rows // LANES)
    for t in range(half_rows // LANES):
        a = jnp.broadcast_to(feed_of[pl.ds(row_at + t, 1), :], (LANES, LANES)).T
        b = jnp.broadcast_to(conv_of[pl.ds(row_at + t, 1), :], (LANES, LANES)).T
        voxel = row * half_rows + t * LANES + iota((LANES, LANES), 0)
        near = 2.0 - (voxel == 0).astype(F32) - (voxel == voxels - 1).astype(F32)
        here = pl.ds(t * LANES, LANES)
        a2, ab = a * a, a * b
        values = (
            STEP * (b - 1.0) - d0 * near, -STEP * a2 - d1 * near, STEP * a2, -STEP * b,
        )
        for i, value in enumerate(values):
            full[i, here, :] = value
            half[i, here, :] = 0.5 * value
        noise[0, here, :] = STEP * (2.0 * a + 2.0 * ab)
        noise[1, here, :] = STEP * (2.0 * ab)
        noise[2, here, :] = STEP * (-2.0 * ab)

    first = cols_at * (panels // 2)
    lane = iota((panels // 2, LANES), 1)
    for t in range(2):
        pick = lane // 2 + (LANES // 2) * t
        for source, target in ((feed_of, ext_a), (conv_of, ext_b)):
            value = source[pl.ds(pl.multiple_of(first, panels // 2), panels // 2), :]
            target[pl.ds(8 + t, panels // 2, stride=2), :] = jnp.take_along_axis(value, pick, axis=1)
    before, after = jnp.maximum(first - 1, 0), jnp.minimum(first + panels // 2, class_rows - 1)
    for source, target in ((feed_of, ext_a), (conv_of, ext_b)):
        value = jnp.broadcast_to(source[pl.ds(before, 1), :], (8, LANES))
        target[0:8, :] = jnp.take_along_axis(value, lane8 // 2 + LANES // 2, axis=1)
        value = jnp.broadcast_to(source[pl.ds(after, 1), :], (8, LANES))
        target[8 + panels : 16 + panels, :] = jnp.take_along_axis(value, lane8 // 2, axis=1)
    shape = ext_a.shape
    lane_e = iota(shape, 1)
    even_e = lane_e % 2 == 0
    a, b = ext_a[...], ext_b[...]
    voxel = cols_at * (panels * LANES // 2) + (iota(shape, 0) - 8) * (LANES // 2) + lane_e // 2
    near = 2.0 - (voxel == 0).astype(F32) - (voxel == voxels - 1).astype(F32)
    d_e = jnp.where(even_e, d0, d1)
    ext_s[...] = STEP * jnp.where(even_e, b - 1.0, -a * a) - d_e * near
    ext_x[...] = STEP * jnp.where(even_e, a * a, -b)

    mid = slice(8, 8 + panels)
    lane = iota((panels, LANES), 1)
    even = lane % 2 == 0
    near, a, b = near[mid], a[mid], b[mid]
    d = jnp.where(even, d0, d1)
    other_d = jnp.where(even, d1, d0)

    def shifted(ref):
        here = ref[mid, :]
        left = pltpu.roll(jnp.where(lane >= LANES - 2, ref[7 : 7 + panels, :], here), 2, 1)
        right = pltpu.roll(jnp.where(lane < 2, ref[9 : 9 + panels, :], here), LANES - 2, 1)
        mate = jnp.where(even, pltpu.roll(here, LANES - 1, 1), pltpu.roll(here, 1, 1))
        return here, mate, jnp.where(even, right, left), jnp.where(even, left, right)

    s, s_mate, s_fore, s_back = shifted(ext_s)
    x, x_mate, x_fore, x_back = shifted(ext_x)
    col[0] = s
    col[1] = x
    col[2] = d
    col[3] = 1.0 + s + 0.5 * (s * s + x * x_mate + d * d * near)
    col[4] = x + 0.5 * x * (s + s_mate)
    col[5] = d + 0.5 * d * (s + s_fore)
    col[6] = d + 0.5 * d * (s + s_back)
    col[7] = 0.5 * d * d
    col[8] = 0.5 * (x * other_d + d * x_fore)
    col[9] = 0.5 * (x * other_d + d * x_back)
    ab = a * b
    same, cross = STEP * (jnp.where(even, 2.0 * a, 0.0) + 2.0 * ab), STEP * (-2.0 * ab)
    col[10] = jnp.where(even, same, cross)
    col[11] = jnp.where(even, cross, same)

    at = iota(code.shape, 1)
    code[...] = (iota(code.shape, 0) - 16 - at) * (1 - 2 * (at % 2))

    def weights(p, _):
        c = [jnp.broadcast_to(col[i, pl.ds(p, 1), :], (16, LANES)) for i in range(10)]
        none = jnp.zeros((16, LANES), F32)
        blank = jnp.zeros((96, 2 * LANES), BF16)
        whi[p, LANES + 16 : 2 * LANES - 16, :] = blank
        wlo[p, LANES + 16 : 2 * LANES - 16, :] = blank
        for i in range(10):
            k = code[16 * i : 16 * i + 16, :]
            z = k == 0, k == 1, k == 2, k == -2
            u = jnp.where(jnp.abs(k) == 4, c[7], none)
            u = jnp.where(k == 3, c[8], u)
            u = jnp.where(k == -1, c[9], u)
            u = jnp.where(z[0], c[3], jnp.where(z[1], c[4], jnp.where(z[2], c[5], jnp.where(z[3], c[6], u))))
            w = jnp.where(z[0], c[0], jnp.where(z[1], c[1], jnp.where(z[2] | z[3], c[2], none)))
            to = 2 * LANES - 16 if i == 0 else LANES if i == 9 else 16 * (i - 1)
            for value, lanes in ((u, slice(0, LANES)), (w, slice(LANES, 2 * LANES))):
                hi, lo = split(value)
                whi[p, to : to + 16, lanes] = hi
                wlo[p, to : to + 16, lanes] = lo
        return 0

    lax.fori_loop(0, panels, weights, 0)

    load(0).wait()
    load(panels - 1).wait()
    lane8 = iota((8, LANES), 1)
    sub8 = iota((8, LANES), 0)
    lane16 = iota((16, LANES), 1)
    for side, panel, start in ((0, 1, 0), (1, panels, LANES - 4)):
        packed = jnp.zeros((16, LANES), F32)
        for g in range(groups):
            piece = vx[panel, PAD + 16 * g : PAD + 16 * g + 16, :]
            turn = (4 * g - start) % LANES
            piece = pltpu.roll(piece, turn, 1) if turn else piece
            packed = jnp.where((lane16 >= 4 * g) & (lane16 < 4 * g + 4), piece, packed)
        send_col[side] = packed

    def wait_load(p, _):
        load(p).wait()
        return 0

    lax.fori_loop(1, panels - 1, wait_load, 0)
    for k in range(panels // 2):
        one, two = 2 * k + 1, 2 * k + 2
        send_row[0, 8 * k : 8 * k + 8, :] = jnp.where(sub8 < 4, vx[one, PAD : PAD + 8, :], vx[two, PAD - 4 : PAD + 4, :])
        end = PAD + rows
        send_row[1, 8 * k : 8 * k + 8, :] = jnp.where(sub8 < 4, vx[one, end - 4 : end + 4, :], vx[two, end - 8 : end, :])

    pl.semaphore_wait(barrier, count)
    tile_rows = 4 * panels

    def remote(i):
        dr, dc = SIDES[i]
        if dc == 0:
            side = 0 if dr < 0 else 1
            source, target = send_row.at[side], got_row.at[1 - side, pl.ds(8, tile_rows), :]
        elif dr == 0:
            side = 0 if dc < 0 else 1
            source, target = send_col.at[side], got_col.at[1 - side]
        else:
            panel = 1 if dc < 0 else panels
            at = PAD if dr < 0 else PAD + rows - 8
            corner = (2 if dr < 0 else 0) + (1 if dc < 0 else 0)
            source, target = vx.at[panel, pl.ds(at, 8), :], got_corner.at[corner]
        return pltpu.make_async_remote_copy(
            src_ref=source, dst_ref=target, send_sem=send_sem.at[i], recv_sem=recv_sem.at[i],
            device_id=(row + dr, cols_at + dc), device_id_type=MESH,
        )

    for i, (dr, dc) in enumerate(SIDES):
        @pl.when(there(dr, dc))
        def _(i=i):
            remote(i).start()

    def split_panel(p):
        for g in range(groups):
            e = vx[p, pl.ds(PAD + 16 * g, 8, stride=2), :]
            o = vx[p, pl.ds(PAD + 16 * g + 1, 8, stride=2), :]
            hi, lo = split(jnp.concatenate([e, o], axis=0))
            high[p, 16 * g : 16 * g + 16, :] = hi
            low[p, 16 * g : 16 * g + 16, :] = lo

    chunk = 128
    left_half = iota((chunk, LANES), 1) < LANES // 2

    def panel_step(p):
        rhs = jnp.concatenate([whi[p - 1], whi[p - 1], wlo[p - 1]], axis=0)
        for q in range(rows // chunk):
            here = pl.ds(chunk * q, chunk)
            hi, lo = high[p, here, :], low[p, here, :]
            edge_hi = jnp.where(left_half, high[p + 1, here, :], high[p - 1, here, :])
            edge_lo = jnp.where(left_half, low[p + 1, here, :], low[p - 1, here, :])
            lhs = jnp.concatenate([hi, edge_hi, lo, edge_lo, hi, edge_hi], axis=1)
            both = jnp.dot(lhs, rhs, preferred_element_type=F32)
            u_ref[p - 1, here, :] = both[:, :LANES]
            w = both[:, LANES:]
            for i in range(chunk // 16):
                g = q * (chunk // 16) + i
                at = PAD + 16 * g
                e, o = vx[p, pl.ds(at, 8, stride=2), :], vx[p, pl.ds(at + 1, 8, stride=2), :]
                e_sum = vx[p, pl.ds(at - 2, 8, stride=2), :] + vx[p, pl.ds(at + 2, 8, stride=2), :]
                o_sum = vx[p, pl.ds(at - 1, 8, stride=2), :] + vx[p, pl.ds(at + 3, 8, stride=2), :]
                c = [half[n, 8 * g : 8 * g + 8, :] for n in range(4)]
                ge[p - 1, PAD + 8 * g : PAD + 8 * g + 8, :] = (
                    e + w[16 * i : 16 * i + 8] + ((c[0] * e + c[2] * o) + (0.5 * d0) * e_sum)
                )
                go[p - 1, PAD + 8 * g : PAD + 8 * g + 8, :] = (
                    o + w[16 * i + 8 : 16 * i + 16] + ((c[1] * o + c[3] * e) + (0.5 * d1) * o_sum)
                )

    split_panel(1)
    split_panel(2)

    def middle(p, _):
        split_panel(p + 1)
        panel_step(p)
        return 0

    lax.fori_loop(2, panels, middle, 0)

    def wait_recv(dr, dc):
        @pl.when(there(-dr, -dc))
        def _():
            remote(SIDES.index((dr, dc))).wait_recv()

    wait_recv(0, 1)
    wait_recv(0, -1)
    for side, panel, start in ((0, 0, LANES - 4), (1, panels + 1, 0)):
        packed = got_col[side]
        for g in range(groups):
            turn = (start - 4 * g) % LANES
            vx[panel, PAD + 16 * g : PAD + 16 * g + 16, :] = pltpu.roll(packed, turn, 1) if turn else packed
        split_panel(panel)

    def outer(i, _):
        panel_step(1 + i * (panels - 1))
        return 0

    lax.fori_loop(0, 2, outer, 0)

    for dr, dc in SIDES:
        if dr:
            wait_recv(dr, dc)
    for side in (0, 1):
        left, right = got_corner[2 * side], got_corner[2 * side + 1]
        if side == 0:
            tile_g[0:8, :] = right
            got_row[side, 0:8, :] = left
            got_row[side, 8 + tile_rows : 16 + tile_rows, :] = tile_g[4:12, :]
        else:
            tile_g[8:16, :] = left
            got_row[side, 0:8, :] = tile_g[4:12, :]
            got_row[side, 8 + tile_rows : 16 + tile_rows, :] = right
    even8 = lane8 % 2 == 0
    upper = sub8 < 4
    species = sub8 % 2 == 0
    for side in (0, 1):
        ok = there(-1, 0) if side == 0 else there(1, 0)
        voxel = jnp.clip(row * half_rows + (-1 if side == 0 else half_rows), 0, voxels - 1)
        pick = lane8 * 0 + voxel % LANES
        a = jnp.broadcast_to(feed_of[pl.ds(voxel // LANES, 1), :], (8, LANES))
        b = jnp.broadcast_to(conv_of[pl.ds(voxel // LANES, 1), :], (8, LANES))
        a = jnp.sum(jnp.where(lane8 == pick, a, 0.0), axis=1, keepdims=True)
        b = jnp.sum(jnp.where(lane8 == pick, b, 0.0), axis=1, keepdims=True)
        end = (voxel == 0) | (voxel == voxels - 1)
        near = jnp.where(end, 1.0, 2.0)
        d_r = jnp.where(species, d0, d1)
        s_r = STEP * jnp.where(species, b - 1.0, -a * a) - d_r * near
        x_r = STEP * jnp.where(species, a * a, -b)
        for k in range(panels // 2):
            at = 8 + 8 * k
            one, two = 2 * k + 1, 2 * k + 2
            tile, left, right = (got_row[side, at + t : at + t + 8, :] for t in (0, -4, 4))
            c_s, c_x, c_d = (
                jnp.where(upper, col[i, 2 * k : 2 * k + 1, :], col[i, 2 * k + 1 : 2 * k + 2, :]) for i in range(3)
            )
            mate = jnp.where(even8, pltpu.roll(tile, LANES - 1, 1), pltpu.roll(tile, 1, 1))
            far = pltpu.roll(jnp.where(lane8 >= LANES - 2, left, tile), 2, 1) + pltpu.roll(
                jnp.where(lane8 < 2, right, tile), LANES - 2, 1
            )
            w = c_s * tile + c_x * mate + c_d * far
            row_mate = jnp.where(species, got_row[side, at + 1 : at + 9, :], got_row[side, at - 1 : at + 7, :])
            if side == 0:
                out = got_row[side, at - 2 : at + 6, :]
                inn = jnp.where(upper, vx[one, PAD - 2 : PAD + 6, :], vx[two, PAD - 6 : PAD + 2, :])
            else:
                out = got_row[side, at + 2 : at + 10, :]
                e = PAD + rows
                inn = jnp.where(upper, vx[one, e - 2 : e + 6, :], vx[two, e - 6 : e + 2, :])
            g = tile + w + 0.5 * (s_r * tile + x_r * row_mate + d_r * (out + inn))
            tile_g[8 + 8 * k : 16 + 8 * k, :] = jnp.where(ok, g, 0.0)
        for k in range(panels // 2):
            for t in (0, 1):
                p, at = 2 * k + t, 8 + 8 * k + 4 * t
                for ref, o, dd in ((ge, 0, d0), (go, 1, d1)):
                    if side == 0:
                        ref[p, 0:8, :] = tile_g[at + 2 + o - 7 : at + 2 + o + 1, :]
                        here, sub, from_ = slice(PAD, PAD + 8), 0, at + 2 + o
                    else:
                        end = PAD + half_rows
                        ref[p, end : end + 8, :] = tile_g[at + o : at + o + 8, :]
                        here, sub, from_ = slice(end - 8, end), 7, at + o - 7
                    ref[p, here, :] += jnp.where(sub8 == sub, (0.5 * dd) * got_row[side, from_ : from_ + 8, :], 0.0)

    row_voxel = row * half_rows
    col_voxel = cols_at * (panels * LANES // 2)

    def add_noise(g, t):
        c = [col[i, pl.ds(t, 1), :] for i in (0, 1, 2, 10, 11)]
        here = pl.ds(pl.multiple_of(8 * g, 8), 8)
        f = [full[i, here, :] for i in range(4)]
        n_e, n_o, n_x = (noise[i, here, :] for i in range(3))
        gap = (col_voxel + t * (LANES // 2) + lane8 // 2) - (row_voxel + 8 * g + sub8)
        on, beside = gap == 0, jnp.abs(gap) == 1
        at = pl.multiple_of(16 * g, 16)
        for start, s_r, x_r, d_r, one, two, mine, mate in (
            (at, f[0], f[2], d0, c[3], c[4], jnp.where(even8, n_e, n_x), jnp.where(even8, n_x, n_e)),
            (at + 8, f[1], f[3], d1, c[4], c[3], jnp.where(even8, n_x, n_o), jnp.where(even8, n_o, n_x)),
        ):
            centre = mine + 0.5 * ((s_r * one + x_r * two) + (c[0] * mine + c[1] * mate))
            side = 0.5 * (d_r * one + c[2] * mine)
            u_ref[t, pl.ds(start, 8), :] += jnp.where(on, centre, jnp.where(beside, side, 0.0))

    near_diagonal = (row_voxel + half_rows >= col_voxel) & (row_voxel <= col_voxel + panels * LANES // 2)

    @pl.when(near_diagonal)
    def _():
        def step(g, _):
            voxel = row_voxel + 8 * g - col_voxel
            t = (voxel + LANES) // (LANES // 2) - 2
            inside = voxel % (LANES // 2)
            for move, ok in ((0, True), (-1, inside == 0), (1, inside == LANES // 2 - 8)):
                @pl.when(ok & (t + move >= 0) & (t + move < panels))
                def _(move=move):
                    add_noise(g, t + move)
            return 0

        lax.fori_loop(0, groups, step, 0)

    for i, (dr, dc) in enumerate(SIDES):
        @pl.when(there(dr, dc))
        def _(i=i):
            remote(i).wait_send()


def finish_kernel(rows, panels, u_ref, ge, go, full, diff, out, stage, sem):
    d0, d1 = diff[0] * STEP, diff[1] * STEP
    groups = rows // 16
    wide = 2

    def store(p):
        return pltpu.make_async_copy(
            stage.at[p], out.at[:, pl.ds(pl.multiple_of(p * LANES, LANES), LANES)], sem.at[p]
        )

    def step(n, _):
        for g in range(groups):
            c = [full[i, 8 * g : 8 * g + 8, :] for i in range(4)]
            for t in range(wide):
                p = n * wide + t
                at = PAD + 8 * g
                e, o = ge[p, at : at + 8, :], go[p, at : at + 8, :]
                e_sum = ge[p, at - 1 : at + 7, :] + ge[p, at + 1 : at + 9, :]
                o_sum = go[p, at - 1 : at + 7, :] + go[p, at + 1 : at + 9, :]
                u_e, u_o = u_ref[p, 16 * g : 16 * g + 8, :], u_ref[p, 16 * g + 8 : 16 * g + 16, :]
                stage[p, pl.ds(16 * g, 8, stride=2), :] = u_e + ((c[0] * e + c[2] * o) + d0 * e_sum)
                stage[p, pl.ds(16 * g + 1, 8, stride=2), :] = u_o + ((c[1] * o + c[3] * e) + d1 * o_sum)
        for t in range(wide):
            store(n * wide + t).start()
        return 0

    lax.fori_loop(0, panels // wide, step, 0)

    def drain(p, _):
        store(p).wait()
        return 0

    lax.fori_loop(0, panels, drain, 0)


def body(covariance, classes, feed_rate, conversion_rate, diffusion):
    rows, cols = covariance.shape
    panels = cols // LANES
    voxels = classes.shape[0]
    half_rows = rows // 2
    vmem = pl.BlockSpec(memory_space=pltpu.VMEM)
    smem = pl.BlockSpec(memory_space=pltpu.SMEM)
    hbm = pl.BlockSpec(memory_space=pl.ANY)
    sizes = (lax.axis_size("row"), lax.axis_size("col"))
    results = [
        pltpu.VMEM((panels, rows, LANES), F32),
        pltpu.VMEM((panels, half_rows + 2 * PAD, LANES), F32),
        pltpu.VMEM((panels, half_rows + 2 * PAD, LANES), F32),
        pltpu.VMEM((4, half_rows, LANES), F32),
    ]
    u, ge, go, full = pl.pallas_call(
        functools.partial(advance_kernel, rows, panels, voxels, *sizes),
        out_shape=results,
        in_specs=[pl.BlockSpec(memory_space=pltpu.HBM), vmem, smem, smem, smem],
        out_specs=[vmem] * 4,
        scratch_shapes=[
            pltpu.VMEM((panels + 2, rows + 2 * PAD, LANES), F32),
            pltpu.VMEM((panels + 2, rows, LANES), BF16),
            pltpu.VMEM((panels + 2, rows, LANES), BF16),
            pltpu.VMEM((panels, 2 * LANES, 2 * LANES), BF16),
            pltpu.VMEM((panels, 2 * LANES, 2 * LANES), BF16),
            pltpu.VMEM((160, LANES), jnp.int32),
            pltpu.VMEM((4, half_rows, LANES), F32),
            pltpu.VMEM((3, half_rows, LANES), F32),
            pltpu.VMEM((voxels // LANES, LANES), F32),
            pltpu.VMEM((voxels // LANES, LANES), F32),
            pltpu.VMEM((panels + 16, LANES), F32),
            pltpu.VMEM((panels + 16, LANES), F32),
            pltpu.VMEM((panels + 16, LANES), F32),
            pltpu.VMEM((panels + 16, LANES), F32),
            pltpu.VMEM((12, panels, LANES), F32),
            pltpu.VMEM((2, 4 * panels, LANES), F32),
            pltpu.VMEM((2, 16, LANES), F32),
            pltpu.VMEM((2, 4 * panels + 16, LANES), F32),
            pltpu.VMEM((2, 16, LANES), F32),
            pltpu.VMEM((4, 8, LANES), F32),
            pltpu.VMEM((4 * panels + 16, LANES), F32),
            pltpu.SemaphoreType.DMA((panels,)),
            pltpu.SemaphoreType.DMA((4,)),
            pltpu.SemaphoreType.DMA((8,)),
            pltpu.SemaphoreType.DMA((8,)),
        ],
        compiler_params=pltpu.CompilerParams(
            collective_id=0, has_side_effects=True, vmem_limit_bytes=24 << 20
        ),
        name="halo_and_columns",
    )(covariance, classes.reshape(voxels // LANES, LANES), feed_rate, conversion_rate, diffusion)
    return pl.pallas_call(
        functools.partial(finish_kernel, rows, panels),
        out_shape=jax.ShapeDtypeStruct((rows, cols), F32),
        in_specs=[vmem] * 4 + [smem],
        out_specs=hbm,
        scratch_shapes=[
            pltpu.VMEM((panels, rows, LANES), F32),
            pltpu.SemaphoreType.DMA((panels,)),
        ],
        compiler_params=pltpu.CompilerParams(vmem_limit_bytes=24 << 20),
        name="rows",
    )(u, ge, go, full, diffusion)


def solution(mesh):
    in_specs = (P("row", "col"), P(), P(), P(), P())
    return jax.shard_map(body, mesh=mesh, in_specs=in_specs, out_specs=P("row", "col"), check_vma=False)
```

time: 107 us -> 23.6 us (0.22)
  the two profiles are of different devices: /device:TPU:129 before, /device:TPU:63 now
where the time goes in v1:
time: 23.6 us; the launch traced here: 23.4 us
  Pallas kernels  18.5 us (78%)
  local copies, waits for them, and re-layouts  4.91 us (21%)
    pallas_call x1, Pallas kernels, body(): pl.pallas_call(functools.partial(advance_kernel, rows, panels, voxels, *s...  15.4 us
    unnamed x10, local copies, waits for them, and re-layouts  4.91 us
    pallas_call x1, Pallas kernels, body(): pl.pallas_call(functools.partial(finish_kernel, rows, panels), out_shape=...  3.07 us

profile of v1, /device:TPU:63, one launch (start us, length us, event | category | flops | bytes accessed | tf_op | source)
XLA Modules:
  0.0 23.4 jit_solution(2930759140846925891)
XLA Ops:
  0.0 0.0 copy-start
  0.0 2.2 %copy-done = f32[512,2048]{1,0:T(8,128)S(1)} copy-done((f32[512,2048]{1,0:T(8,128)S(1)}, f32[512,2048]{1,0:T(8,128)}, u32[]{:S(2)}) %copy-start) | copy-done | bytes 4194328
  2.2 0.0 copy-start.1
  2.2 0.8 %copy-done.1 = s32[8192]{0:T(1024)S(1)} copy-done((s32[8192]{0:T(1024)S(1)}, s32[8192]{0:T(1024)}, u32[]{:S(2)}) %copy-start.1) | copy-done | bytes 32792
  2.9 0.0 copy-start.2
  2.9 0.7 %copy-done.2 = f32[2]{0:T(128)S(1)} copy-done((f32[2]{0:T(128)S(1)}, f32[2]{0:T(128)}, u32[]{:S(2)}) %copy-start.2) | copy-done | bytes 32
  3.6 0.0 copy-start.3
  3.6 0.7 %copy-done.3 = f32[16]{0:T(128)S(1)} copy-done((f32[16]{0:T(128)S(1)}, f32[16]{0:T(128)}, u32[]{:S(2)}) %copy-start.3) | copy-done | bytes 88
  4.3 0.0 copy-start.4
  4.3 0.7 %copy-done.4 = f32[16]{0:T(128)S(1)} copy-done((f32[16]{0:T(128)S(1)}, f32[16]{0:T(128)}, u32[]{:S(2)}) %copy-start.4) | copy-done | bytes 88
  4.9 15.4 %halo_and_columns.1 = (f32[16,512,128]{2,1,0:T(8,128)S(1)}, f32[16,272,128]{2,1,0:T(8,128)S(1)}, f32[16,272,128]{2,1,0:T(8,128)S(1)}, f32[4,256,128]{2,1,0:T(8,128)S(1)}) custom-call(f32[512,2048]{1,0:T(8,128)S(1)} %copy-done, s32[64,128]{1,0:T(8,128)S(1)} %bitcast.1, f32[16]{0:T(128)S(1)} %copy-done.3, f32[16]{0:T(128)S(1)} %copy-done.4, f32[2]{0:T(128)S(1)} %copy-done.2), custom_call_target="tpu_custom_call" | custom-call | tf_op jit(solution)/shard_map/halo_and_columns/pallas_call | solution.py:471
  20.3 3.1 %rows.1 = f32[512,2048]{1,0:T(8,128)} custom-call(f32[16,512,128]{2,1,0:T(8,128)S(1)} %get-tuple-element.9.u_ref, f32[16,272,128]{2,1,0:T(8,128)S(1)} %get-tuple-element.10.ge, f32[16,272,128]{2,1,0:T(8,128)S(1)} %get-tuple-element.11.go, f32[4,256,128]{2,1,0:T(8,128)S(1)} %get-tuple-element.12.full, f32[2]{0:T(128)S(1)} %copy-done.2), custom_call_target="tpu_custom_call" | custom-call | tf_op jit(solution)/shard_map/rows/pallas_call | solution.py:508
Async XLA Ops:
  0.0 2.2 %copy-start = (f32[512,2048]{1,0:T(8,128)S(1)}, f32[512,2048]{1,0:T(8,128)}, u32[]{:S(2)}) copy-start(f32[512,2048]{1,0:T(8,128)} %cov.1) | copy-start | bytes 12582916
  2.2 0.8 %copy-start.1 = (s32[8192]{0:T(1024)S(1)}, s32[8192]{0:T(1024)}, u32[]{:S(2)}) copy-start(s32[8192]{0:T(1024)} %param.6) | copy-start | bytes 98308
  2.9 0.7 %copy-start.2 = (f32[2]{0:T(128)S(1)}, f32[2]{0:T(128)}, u32[]{:S(2)}) copy-start(f32[2]{0:T(128)} %diff.3) | copy-start | bytes 28
  3.6 0.7 %copy-start.3 = (f32[16]{0:T(128)S(1)}, f32[16]{0:T(128)}, u32[]{:S(2)}) copy-start(f32[16]{0:T(128)} %feed.1) | copy-start | bytes 196
  4.3 0.7 %copy-start.4 = (f32[16]{0:T(128)S(1)}, f32[16]{0:T(128)}, u32[]{:S(2)}) copy-start(f32[16]{0:T(128)} %conv.1) | copy-start | bytes 196

commit v2 on v1

--- a/solution.py
+++ b/solution.py
@@ -26,17 +26,15 @@
 
 def advance_kernel(
     rows, panels, voxels, grid_rows, grid_cols,
-    cov, classes, feed, conv, diff,
-    u_ref, ge, go, full,
-    vx, high, low, whi, wlo, code, half, noise, feed_of, conv_of, ext_s, ext_x, ext_a, ext_b, col,
-    send_row, send_col, got_row, got_col, got_corner, tile_g,
-    load_sem, edge_sem, send_sem, recv_sem,
+    cov, classes_in, feed_in, conv_in, diff_in,
+    u_ref, ge, go, full, spread,
+    vx, high, low, whi, wlo, w_one, w_two, half, noise, feed_of, conv_of, ext_s, ext_x, ext_a, ext_b, col,
+    classes, feed, conv, diff, edge, send_row, send_col, got_row, got_col, got_corner, tile_g,
+    load_sem, small_sem, send_sem, recv_sem,
 ):
     row, cols_at = lax.axis_index("row"), lax.axis_index("col")
     groups = rows // 16
     half_rows = rows // 2
-    d0, d1 = diff[0] * STEP, diff[1] * STEP
-
     def there(dr, dc):
         ok = None
         for at, step, size in ((row, dr, grid_rows), (cols_at, dc, grid_cols)):
@@ -45,16 +43,15 @@
                 ok = one if ok is None else ok & one
         return ok
 
-    barrier = pltpu.get_barrier_semaphore()
-    count = jnp.int32(0)
-    for dr, dc in SIDES:
-        ok = there(dr, dc)
-        count += ok.astype(jnp.int32)
-
-        @pl.when(ok)
-        def _(dr=dr, dc=dc):
-            pl.semaphore_signal(barrier, inc=1, device_id=(row + dr, cols_at + dc), device_id_type=MESH)
-
+    small = [
+        pltpu.make_async_copy(a, b, small_sem.at[n])
+        for n, (a, b) in enumerate((
+            (classes_in, classes), (feed_in, feed), (conv_in, conv), (diff_in, diff),
+            (cov.at[pl.ds(0, 8), :], edge.at[0]), (cov.at[pl.ds(rows - 8, 8), :], edge.at[1]),
+        ))
+    ]
+    for copy in small:
+        copy.start()
     def load(p):
         return pltpu.make_async_copy(
             cov.at[:, pl.ds(pl.multiple_of(p * LANES, LANES), LANES)],
@@ -70,6 +67,16 @@
         return 0
 
     lax.fori_loop(1, panels - 1, start_load, 0)
+
+    barrier = pltpu.get_barrier_semaphore()
+    count = jnp.int32(0)
+    for dr, dc in SIDES:
+        ok = there(dr, dc)
+        count += ok.astype(jnp.int32)
+
+        @pl.when(ok)
+        def _(dr=dr, dc=dc):
+            pl.semaphore_signal(barrier, inc=1, device_id=(row + dr, cols_at + dc), device_id_type=MESH)
 
     zero = jnp.zeros((8, LANES), F32)
     for p in range(panels):
@@ -88,6 +95,11 @@
         def _(i=i):
             got_corner[i] = zero
 
+    for copy in small[:4]:
+        copy.wait()
+    d0, d1 = diff[0] * STEP, diff[1] * STEP
+    spread[0] = jnp.full((8, LANES), d0, F32)
+    spread[1] = jnp.full((8, LANES), d1, F32)
     ids = classes[...]
     a_all, b_all = jnp.zeros(ids.shape, F32), jnp.zeros(ids.shape, F32)
     for k in range(feed.shape[0]):
@@ -170,32 +182,6 @@
     col[10] = jnp.where(even, same, cross)
     col[11] = jnp.where(even, cross, same)
 
-    at = iota(code.shape, 1)
-    code[...] = (iota(code.shape, 0) - 16 - at) * (1 - 2 * (at % 2))
-
-    def weights(p, _):
-        c = [jnp.broadcast_to(col[i, pl.ds(p, 1), :], (16, LANES)) for i in range(10)]
-        none = jnp.zeros((16, LANES), F32)
-        blank = jnp.zeros((96, 2 * LANES), BF16)
-        whi[p, LANES + 16 : 2 * LANES - 16, :] = blank
-        wlo[p, LANES + 16 : 2 * LANES - 16, :] = blank
-        for i in range(10):
-            k = code[16 * i : 16 * i + 16, :]
-            z = k == 0, k == 1, k == 2, k == -2
-            u = jnp.where(jnp.abs(k) == 4, c[7], none)
-            u = jnp.where(k == 3, c[8], u)
-            u = jnp.where(k == -1, c[9], u)
-            u = jnp.where(z[0], c[3], jnp.where(z[1], c[4], jnp.where(z[2], c[5], jnp.where(z[3], c[6], u))))
-            w = jnp.where(z[0], c[0], jnp.where(z[1], c[1], jnp.where(z[2] | z[3], c[2], none)))
-            to = 2 * LANES - 16 if i == 0 else LANES if i == 9 else 16 * (i - 1)
-            for value, lanes in ((u, slice(0, LANES)), (w, slice(LANES, 2 * LANES))):
-                hi, lo = split(value)
-                whi[p, to : to + 16, lanes] = hi
-                wlo[p, to : to + 16, lanes] = lo
-        return 0
-
-    lax.fori_loop(0, panels, weights, 0)
-
     load(0).wait()
     load(panels - 1).wait()
     lane8 = iota((8, LANES), 1)
@@ -210,16 +196,12 @@
             packed = jnp.where((lane16 >= 4 * g) & (lane16 < 4 * g + 4), piece, packed)
         send_col[side] = packed
 
-    def wait_load(p, _):
-        load(p).wait()
-        return 0
-
-    lax.fori_loop(1, panels - 1, wait_load, 0)
+    small[4].wait()
+    small[5].wait()
     for k in range(panels // 2):
-        one, two = 2 * k + 1, 2 * k + 2
-        send_row[0, 8 * k : 8 * k + 8, :] = jnp.where(sub8 < 4, vx[one, PAD : PAD + 8, :], vx[two, PAD - 4 : PAD + 4, :])
-        end = PAD + rows
-        send_row[1, 8 * k : 8 * k + 8, :] = jnp.where(sub8 < 4, vx[one, end - 4 : end + 4, :], vx[two, end - 8 : end, :])
+        one, two = (slice(LANES * (2 * k + t), LANES * (2 * k + t + 1)) for t in (0, 1))
+        send_row[0, 8 * k : 8 * k + 8, :] = jnp.where(sub8 < 4, edge[0, :, one], pltpu.roll(edge[0, :, two], 4, 0))
+        send_row[1, 8 * k : 8 * k + 8, :] = jnp.where(sub8 < 4, pltpu.roll(edge[1, :, one], 4, 0), edge[1, :, two])
 
     pl.semaphore_wait(barrier, count)
     tile_rows = 4 * panels
@@ -233,10 +215,9 @@
             side = 0 if dc < 0 else 1
             source, target = send_col.at[side], got_col.at[1 - side]
         else:
-            panel = 1 if dc < 0 else panels
-            at = PAD if dr < 0 else PAD + rows - 8
+            lanes = pl.ds(0 if dc < 0 else (panels - 1) * LANES, LANES)
             corner = (2 if dr < 0 else 0) + (1 if dc < 0 else 0)
-            source, target = vx.at[panel, pl.ds(at, 8), :], got_corner.at[corner]
+            source, target = edge.at[0 if dr < 0 else 1, :, lanes], got_corner.at[corner]
         return pltpu.make_async_remote_copy(
             src_ref=source, dst_ref=target, send_sem=send_sem.at[i], recv_sem=recv_sem.at[i],
             device_id=(row + dr, cols_at + dc), device_id_type=MESH,
@@ -246,6 +227,43 @@
         @pl.when(there(dr, dc))
         def _(i=i):
             remote(i).start()
+
+    at16 = iota((16, LANES), 1)
+    in16 = iota((16, LANES), 0)
+    owner = (at16 + 4) // 32, (at16 + 20) // 32
+    codes = [
+        (16 * tile + in16 - at16) * (1 - 2 * (at16 % 2)) for tile in (2 * owner[0], 2 * owner[1] - 1)
+    ]
+    wide_at = iota((16, 2 * LANES), 1) % LANES
+    wide_owner = (wide_at + 4) // 32, (wide_at + 20) // 32
+    blank = jnp.zeros((16, 2 * LANES), BF16)
+
+    def weights(p, _):
+        c = [jnp.broadcast_to(col[i, pl.ds(p, 1), :], (16, LANES)) for i in range(10)]
+        none = jnp.zeros((16, LANES), F32)
+        pairs = []
+        for k in codes:
+            z = k == 0, k == 1, k == 2, k == -2
+            u = jnp.where(jnp.abs(k) == 4, c[7], none)
+            u = jnp.where(k == 3, c[8], u)
+            u = jnp.where(k == -1, c[9], u)
+            u = jnp.where(z[0], c[3], jnp.where(z[1], c[4], jnp.where(z[2], c[5], jnp.where(z[3], c[6], u))))
+            w = jnp.where(z[0], c[0], jnp.where(z[1], c[1], jnp.where(z[2] | z[3], c[2], none)))
+            pairs.append(split(jnp.concatenate([u, w], axis=1)))
+
+        def tile(i, part):
+            odd = i % 2
+            return jnp.where(wide_owner[odd] == (i + odd) // 2, pairs[odd][part], blank)
+
+        for i in range(8):
+            whi[p, 16 * i : 16 * i + 16, :] = tile(i, 0)
+            wlo[p, 16 * i : 16 * i + 16, :] = tile(i, 1)
+        before, after = [tile(-1, part) for part in (0, 1)], [tile(8, part) for part in (0, 1)]
+        for i, value in enumerate((after[0], before[0], after[0], before[1], after[1], blank, blank, before[0])):
+            wlo[p, LANES + 16 * i : LANES + 16 * i + 16, :] = value
+        return 0
+
+    lax.fori_loop(0, panels, weights, 0)
 
     def split_panel(p):
         for g in range(groups):
@@ -255,43 +273,61 @@
             high[p, 16 * g : 16 * g + 16, :] = hi
             low[p, 16 * g : 16 * g + 16, :] = lo
 
-    chunk = 128
-    left_half = iota((chunk, LANES), 1) < LANES // 2
-
-    def panel_step(p):
+    split_panel(1)
+    split_panel(panels)
+
+    def next_panel(p, _):
+        load(p - 1).wait()
+        split_panel(p)
+        return 0
+
+    lax.fori_loop(2, panels, next_panel, 0)
+
+    at_rows = iota((rows, LANES), 1)
+    next_lanes = at_rows < LANES // 2
+    low_lanes = (at_rows >= 16) & (at_rows < 48)
+    again_lanes = (at_rows >= 48) & (at_rows < 80)
+
+    def columns(p, w_ref):
+        hi, lo = high[p], low[p]
+        edge_hi = jnp.where(next_lanes, high[p + 1], high[p - 1])
+        edge_lo = jnp.where(next_lanes, low[p + 1], low[p - 1])
+        edges = jnp.where(
+            low_lanes, pltpu.roll(edge_lo, 32, 1), jnp.where(again_lanes, pltpu.roll(edge_hi, 64, 1), edge_hi)
+        )
+        lhs = jnp.concatenate([hi, lo, hi, edges], axis=1)
         rhs = jnp.concatenate([whi[p - 1], whi[p - 1], wlo[p - 1]], axis=0)
-        for q in range(rows // chunk):
-            here = pl.ds(chunk * q, chunk)
-            hi, lo = high[p, here, :], low[p, here, :]
-            edge_hi = jnp.where(left_half, high[p + 1, here, :], high[p - 1, here, :])
-            edge_lo = jnp.where(left_half, low[p + 1, here, :], low[p - 1, here, :])
-            lhs = jnp.concatenate([hi, edge_hi, lo, edge_lo, hi, edge_hi], axis=1)
-            both = jnp.dot(lhs, rhs, preferred_element_type=F32)
-            u_ref[p - 1, here, :] = both[:, :LANES]
-            w = both[:, LANES:]
-            for i in range(chunk // 16):
-                g = q * (chunk // 16) + i
-                at = PAD + 16 * g
-                e, o = vx[p, pl.ds(at, 8, stride=2), :], vx[p, pl.ds(at + 1, 8, stride=2), :]
-                e_sum = vx[p, pl.ds(at - 2, 8, stride=2), :] + vx[p, pl.ds(at + 2, 8, stride=2), :]
-                o_sum = vx[p, pl.ds(at - 1, 8, stride=2), :] + vx[p, pl.ds(at + 3, 8, stride=2), :]
-                c = [half[n, 8 * g : 8 * g + 8, :] for n in range(4)]
-                ge[p - 1, PAD + 8 * g : PAD + 8 * g + 8, :] = (
-                    e + w[16 * i : 16 * i + 8] + ((c[0] * e + c[2] * o) + (0.5 * d0) * e_sum)
-                )
-                go[p - 1, PAD + 8 * g : PAD + 8 * g + 8, :] = (
-                    o + w[16 * i + 8 : 16 * i + 16] + ((c[1] * o + c[3] * e) + (0.5 * d1) * o_sum)
-                )
-
-    split_panel(1)
-    split_panel(2)
-
-    def middle(p, _):
-        split_panel(p + 1)
-        panel_step(p)
+        both = jnp.dot(lhs, rhs, preferred_element_type=F32)
+        u_ref[p - 1] = both[:, :LANES]
+        w_ref[...] = both[:, LANES:]
+
+    def own_rows(p, w_ref):
+        for g in range(groups):
+            at = PAD + 16 * g
+            e, o = vx[p, pl.ds(at, 8, stride=2), :], vx[p, pl.ds(at + 1, 8, stride=2), :]
+            e_sum = vx[p, pl.ds(at - 2, 8, stride=2), :] + vx[p, pl.ds(at + 2, 8, stride=2), :]
+            o_sum = vx[p, pl.ds(at - 1, 8, stride=2), :] + vx[p, pl.ds(at + 3, 8, stride=2), :]
+            c = [half[n, 8 * g : 8 * g + 8, :] for n in range(4)]
+            ge[p - 1, PAD + 8 * g : PAD + 8 * g + 8, :] = (
+                e + w_ref[16 * g : 16 * g + 8, :] + ((c[0] * e + c[2] * o) + (0.5 * d0) * e_sum)
+            )
+            go[p - 1, PAD + 8 * g : PAD + 8 * g + 8, :] = (
+                o + w_ref[16 * g + 8 : 16 * g + 16, :] + ((c[1] * o + c[3] * e) + (0.5 * d1) * o_sum)
+            )
+
+    columns(2, w_one)
+
+    def middle(i, _):
+        p = 3 + 2 * i
+        own_rows(p - 1, w_one)
+        columns(p, w_two)
+        own_rows(p, w_two)
+        columns(p + 1, w_one)
         return 0
 
-    lax.fori_loop(2, panels, middle, 0)
+    lax.fori_loop(0, (panels - 4) // 2, middle, 0)
+    own_rows(panels - 2, w_one)
+    columns(panels - 1, w_two)
 
     def wait_recv(dr, dc):
         @pl.when(there(-dr, -dc))
@@ -307,11 +343,11 @@
             vx[panel, PAD + 16 * g : PAD + 16 * g + 16, :] = pltpu.roll(packed, turn, 1) if turn else packed
         split_panel(panel)
 
-    def outer(i, _):
-        panel_step(1 + i * (panels - 1))
-        return 0
-
-    lax.fori_loop(0, 2, outer, 0)
+    own_rows(panels - 1, w_two)
+    columns(1, w_one)
+    own_rows(1, w_one)
+    columns(panels, w_two)
+    own_rows(panels, w_two)
 
     for dr, dc in SIDES:
         if dr:
@@ -377,40 +413,43 @@
                         here, sub, from_ = slice(end - 8, end), 7, at + o - 7
                     ref[p, here, :] += jnp.where(sub8 == sub, (0.5 * dd) * got_row[side, from_ : from_ + 8, :], 0.0)
 
-    row_voxel = row * half_rows
-    col_voxel = cols_at * (panels * LANES // 2)
-
-    def add_noise(g, t):
+    per_panel = LANES // 16
+
+    def add_noise(g, t, move):
         c = [col[i, pl.ds(t, 1), :] for i in (0, 1, 2, 10, 11)]
-        here = pl.ds(pl.multiple_of(8 * g, 8), 8)
+        here = slice(8 * g, 8 * g + 8)
         f = [full[i, here, :] for i in range(4)]
         n_e, n_o, n_x = (noise[i, here, :] for i in range(3))
-        gap = (col_voxel + t * (LANES // 2) + lane8 // 2) - (row_voxel + 8 * g + sub8)
+        gap = (move * (LANES // 2) + lane8 // 2) - (8 * (g % per_panel) + sub8)
         on, beside = gap == 0, jnp.abs(gap) == 1
-        at = pl.multiple_of(16 * g, 16)
         for start, s_r, x_r, d_r, one, two, mine, mate in (
-            (at, f[0], f[2], d0, c[3], c[4], jnp.where(even8, n_e, n_x), jnp.where(even8, n_x, n_e)),
-            (at + 8, f[1], f[3], d1, c[4], c[3], jnp.where(even8, n_x, n_o), jnp.where(even8, n_o, n_x)),
+            (16 * g, f[0], f[2], d0, c[3], c[4], jnp.where(even8, n_e, n_x), jnp.where(even8, n_x, n_e)),
+            (16 * g + 8, f[1], f[3], d1, c[4], c[3], jnp.where(even8, n_x, n_o), jnp.where(even8, n_o, n_x)),
         ):
             centre = mine + 0.5 * ((s_r * one + x_r * two) + (c[0] * mine + c[1] * mate))
             side = 0.5 * (d_r * one + c[2] * mine)
-            u_ref[t, pl.ds(start, 8), :] += jnp.where(on, centre, jnp.where(beside, side, 0.0))
-
-    near_diagonal = (row_voxel + half_rows >= col_voxel) & (row_voxel <= col_voxel + panels * LANES // 2)
-
-    @pl.when(near_diagonal)
+            u_ref[t, start : start + 8, :] += jnp.where(on, centre, jnp.where(beside, side, 0.0))
+
+    ratio = panels * LANES // rows
+    first_panel = (row - cols_at * ratio) * (rows // LANES)
+
+    @pl.when((first_panel >= 0) & (first_panel < panels))
     def _():
-        def step(g, _):
-            voxel = row_voxel + 8 * g - col_voxel
-            t = (voxel + LANES) // (LANES // 2) - 2
-            inside = voxel % (LANES // 2)
-            for move, ok in ((0, True), (-1, inside == 0), (1, inside == LANES // 2 - 8)):
-                @pl.when(ok & (t + move >= 0) & (t + move < panels))
-                def _(move=move):
-                    add_noise(g, t + move)
-            return 0
-
-        lax.fori_loop(0, groups, step, 0)
+        for g in range(groups):
+            t = first_panel + g // per_panel
+            add_noise(g, t, 0)
+            if g % per_panel == 0 and g:
+                add_noise(g, t - 1, -1)
+            if g % per_panel == per_panel - 1 and g < groups - 1:
+                add_noise(g, t + 1, 1)
+
+    @pl.when((first_panel >= 1) & (first_panel <= panels))
+    def _():
+        add_noise(0, first_panel - 1, -1)
+
+    @pl.when((first_panel + rows // LANES >= 0) & (first_panel + rows // LANES < panels))
+    def _():
+        add_noise(groups - 1, first_panel + rows // LANES, 1)
 
     for i, (dr, dc) in enumerate(SIDES):
         @pl.when(there(dr, dc))
@@ -418,10 +457,10 @@
             remote(i).wait_send()
 
 
-def finish_kernel(rows, panels, u_ref, ge, go, full, diff, out, stage, sem):
-    d0, d1 = diff[0] * STEP, diff[1] * STEP
+def finish_kernel(rows, panels, u_ref, ge, go, full, spread, out, stage, sem):
+    d0, d1 = spread[0], spread[1]
     groups = rows // 16
-    wide = 2
+    wide = 4
 
     def store(p):
         return pltpu.make_async_copy(
@@ -459,27 +498,28 @@
     voxels = classes.shape[0]
     half_rows = rows // 2
     vmem = pl.BlockSpec(memory_space=pltpu.VMEM)
-    smem = pl.BlockSpec(memory_space=pltpu.SMEM)
     hbm = pl.BlockSpec(memory_space=pl.ANY)
     sizes = (lax.axis_size("row"), lax.axis_size("col"))
-    results = [
-        pltpu.VMEM((panels, rows, LANES), F32),
-        pltpu.VMEM((panels, half_rows + 2 * PAD, LANES), F32),
-        pltpu.VMEM((panels, half_rows + 2 * PAD, LANES), F32),
-        pltpu.VMEM((4, half_rows, LANES), F32),
-    ]
-    u, ge, go, full = pl.pallas_call(
+    inputs = (covariance, classes.reshape(voxels // LANES, LANES), feed_rate, conversion_rate, diffusion)
+    results = pl.pallas_call(
         functools.partial(advance_kernel, rows, panels, voxels, *sizes),
-        out_shape=results,
-        in_specs=[pl.BlockSpec(memory_space=pltpu.HBM), vmem, smem, smem, smem],
-        out_specs=[vmem] * 4,
+        out_shape=[
+            pltpu.VMEM((panels, rows, LANES), F32),
+            pltpu.VMEM((panels, half_rows + 2 * PAD, LANES), F32),
+            pltpu.VMEM((panels, half_rows + 2 * PAD, LANES), F32),
+            pltpu.VMEM((4, half_rows, LANES), F32),
+            pltpu.VMEM((2, 8, LANES), F32),
+        ],
+        in_specs=[hbm] * 5,
+        out_specs=[vmem] * 5,
         scratch_shapes=[
             pltpu.VMEM((panels + 2, rows + 2 * PAD, LANES), F32),
             pltpu.VMEM((panels + 2, rows, LANES), BF16),
             pltpu.VMEM((panels + 2, rows, LANES), BF16),
+            pltpu.VMEM((panels, LANES, 2 * LANES), BF16),
             pltpu.VMEM((panels, 2 * LANES, 2 * LANES), BF16),
-            pltpu.VMEM((panels, 2 * LANES, 2 * LANES), BF16),
-            pltpu.VMEM((160, LANES), jnp.int32),
+            pltpu.VMEM((rows, LANES), F32),
+            pltpu.VMEM((rows, LANES), F32),
             pltpu.VMEM((4, half_rows, LANES), F32),
             pltpu.VMEM((3, half_rows, LANES), F32),
             pltpu.VMEM((voxels // LANES, LANES), F32),
@@ -489,6 +529,11 @@
             pltpu.VMEM((panels + 16, LANES), F32),
             pltpu.VMEM((panels + 16, LANES), F32),
             pltpu.VMEM((12, panels, LANES), F32),
+            pltpu.VMEM((voxels // LANES, LANES), jnp.int32),
+            pltpu.SMEM(feed_rate.shape, F32),
+            pltpu.SMEM(conversion_rate.shape, F32),
+            pltpu.SMEM(diffusion.shape, F32),
+            pltpu.VMEM((2, 8, cols), F32),
             pltpu.VMEM((2, 4 * panels, LANES), F32),
             pltpu.VMEM((2, 16, LANES), F32),
             pltpu.VMEM((2, 4 * panels + 16, LANES), F32),
@@ -496,19 +541,19 @@
             pltpu.VMEM((4, 8, LANES), F32),
             pltpu.VMEM((4 * panels + 16, LANES), F32),
             pltpu.SemaphoreType.DMA((panels,)),
-            pltpu.SemaphoreType.DMA((4,)),
+            pltpu.SemaphoreType.DMA((6,)),
             pltpu.SemaphoreType.DMA((8,)),
             pltpu.SemaphoreType.DMA((8,)),
         ],
         compiler_params=pltpu.CompilerParams(
-            collective_id=0, has_side_effects=True, vmem_limit_bytes=24 << 20
+            collective_id=0, has_side_effects=True, vmem_limit_bytes=32 << 20
         ),
         name="halo_and_columns",
-    )(covariance, classes.reshape(voxels // LANES, LANES), feed_rate, conversion_rate, diffusion)
+    )(*(pltpu.with_memory_space_constraint(x, pltpu.HBM) for x in inputs))
     return pl.pallas_call(
         functools.partial(finish_kernel, rows, panels),
         out_shape=jax.ShapeDtypeStruct((rows, cols), F32),
-        in_specs=[vmem] * 4 + [smem],
+        in_specs=[vmem] * 5,
         out_specs=hbm,
         scratch_shapes=[
             pltpu.VMEM((panels, rows, LANES), F32),
@@ -516,7 +561,7 @@
         ],
         compiler_params=pltpu.CompilerParams(vmem_limit_bytes=24 << 20),
         name="rows",
-    )(u, ge, go, full, diffusion)
+    )(*results)
 
 
 def solution(mesh):

time: 23.6 us -> 16.1 us (0.68)
  local copies, waits for them, and re-layouts: 4.91 us -> 0 us
  Pallas kernels: 18.5 us -> 16 us
    unnamed x10 -> x0, local copies, waits for them, and re-layouts: 4.91 us -> none
    pallas_call x1, Pallas kernels: 15.4 us -> 13.6 us  [body(): pl.pallas_call(functools.partial(advance_kernel, rows, panels, voxels, *s...]
    pallas_call x1, Pallas kernels: 3.07 us -> 2.43 us  [body(): pl.pallas_call(functools.partial(finish_kernel, rows, panels), out_shape=...]
where the time goes in v2:
time: 16.1 us; the launch traced here: 16 us
  Pallas kernels  16 us (99%)
    pallas_call x1, Pallas kernels, body(): pl.pallas_call(functools.partial(advance_kernel, rows, panels, voxels, *s...  13.6 us
    pallas_call x1, Pallas kernels, body(): pl.pallas_call(functools.partial(finish_kernel, rows, panels), out_shape=...  2.43 us

profile of v2, /device:TPU:63, one launch (start us, length us, event | category | flops | bytes accessed | tf_op | source)
XLA Modules:
  0.0 16.0 jit_solution(8259638188028865281)
XLA Ops:
  0.0 13.6 %halo_and_columns.1 = (f32[16,512,128]{2,1,0:T(8,128)S(1)}, f32[16,272,128]{2,1,0:T(8,128)S(1)}, f32[16,272,128]{2,1,0:T(8,128)S(1)}, f32[4,256,128]{2,1,0:T(8,128)S(1)}, f32[2,8,128]{2,1,0:T(8,128)S(1)}) custom-call(f32[512,2048]{1,0:T(8,128)} %cov.1, s32[64,128]{1,0:T(8,128)} %bitcast.1, f32[16]{0:T(128)} %feed_in.1, f32[16]{0:T(128)} %conv_in.1, f32[2]{0:T(128)} %diff_in.1), custom_call_target="tpu_custom_call" | custom-call | tf_op jit(solution)/shard_map/halo_and_columns/pallas_call | solution.py:504
  13.6 2.4 %rows.1 = f32[512,2048]{1,0:T(8,128)} custom-call(f32[16,512,128]{2,1,0:T(8,128)S(1)} %get-tuple-element.10.u_ref, f32[16,272,128]{2,1,0:T(8,128)S(1)} %get-tuple-element.11.ge, f32[16,272,128]{2,1,0:T(8,128)S(1)} %get-tuple-element.12.go, f32[4,256,128]{2,1,0:T(8,128)S(1)} %get-tuple-element.13.full, f32[2,8,128]{2,1,0:T(8,128)S(1)} %get-tuple-element.14.spread), custom_call_target="tpu_custom_call" | custom-call | tf_op jit(solution)/shard_map/rows/pallas_call | solution.py:553

commit v3 on v2

--- a/solution.py
+++ b/solution.py
@@ -27,9 +27,9 @@
 def advance_kernel(
     rows, panels, voxels, grid_rows, grid_cols,
     cov, classes_in, feed_in, conv_in, diff_in,
-    u_ref, ge, go, full, spread,
+    stage, u_edge, ge, go, full, spread, halo, inner, halo_col, halo_row,
     vx, high, low, whi, wlo, w_one, w_two, half, noise, feed_of, conv_of, ext_s, ext_x, ext_a, ext_b, col,
-    classes, feed, conv, diff, edge, send_row, send_col, got_row, got_col, got_corner, tile_g,
+    classes, feed, conv, diff, edge, send_row, send_col, got_row, got_col, got_corner,
     load_sem, small_sem, send_sem, recv_sem,
 ):
     row, cols_at = lax.axis_index("row"), lax.axis_index("col")
@@ -42,6 +42,18 @@
                 one = (at + step >= 0) & (at + step < size)
                 ok = one if ok is None else ok & one
         return ok
+
+    barrier = pltpu.get_barrier_semaphore()
+    count = jnp.int32(0)
+    for dr, dc in SIDES:
+        ok = there(dr, dc)
+        count += ok.astype(jnp.int32)
+
+        @pl.when(ok)
+        def _(dr=dr, dc=dc):
+            pl.semaphore_signal(barrier, inc=1, device_id=(row + dr, cols_at + dc), device_id_type=MESH)
+
+    distant = (row == grid_rows // 2 - 1) | (row == grid_rows // 2)
 
     small = [
         pltpu.make_async_copy(a, b, small_sem.at[n])
@@ -68,32 +80,16 @@
 
     lax.fori_loop(1, panels - 1, start_load, 0)
 
-    barrier = pltpu.get_barrier_semaphore()
-    count = jnp.int32(0)
-    for dr, dc in SIDES:
-        ok = there(dr, dc)
-        count += ok.astype(jnp.int32)
-
-        @pl.when(ok)
-        def _(dr=dr, dc=dc):
-            pl.semaphore_signal(barrier, inc=1, device_id=(row + dr, cols_at + dc), device_id_type=MESH)
-
     zero = jnp.zeros((8, LANES), F32)
     for p in range(panels):
         vx[p + 1, 0:PAD, :] = zero
         vx[p + 1, PAD + rows : 2 * PAD + rows, :] = zero
-    for i, (step, at) in enumerate(((1, 0), (-1, grid_rows - 1))):
-        @pl.when(row == at)
-        def _(i=i):
-            got_row[i] = jnp.zeros(got_row.shape[1:], F32)
     for i, at in enumerate((0, grid_cols - 1)):
         @pl.when(cols_at == at)
         def _(i=i):
             got_col[i] = jnp.zeros(got_col.shape[1:], F32)
-    for i, (dr, dc) in enumerate(((-1, -1), (-1, 1), (1, -1), (1, 1))):
-        @pl.when(jnp.logical_not(there(dr, dc)))
-        def _(i=i):
             got_corner[i] = zero
+            got_corner[2 + i] = zero
 
     for copy in small[:4]:
         copy.wait()
@@ -203,30 +199,35 @@
         send_row[0, 8 * k : 8 * k + 8, :] = jnp.where(sub8 < 4, edge[0, :, one], pltpu.roll(edge[0, :, two], 4, 0))
         send_row[1, 8 * k : 8 * k + 8, :] = jnp.where(sub8 < 4, pltpu.roll(edge[1, :, one], 4, 0), edge[1, :, two])
 
-    pl.semaphore_wait(barrier, count)
     tile_rows = 4 * panels
+
+    def landing(i):
+        dr, dc = SIDES[i]
+        if dc == 0:
+            return got_row.at[0 if dr > 0 else 1, pl.ds(8, tile_rows), :]
+        if dr == 0:
+            return got_col.at[0 if dc > 0 else 1]
+        return got_corner.at[(2 if dr < 0 else 0) + (1 if dc < 0 else 0)]
 
     def remote(i):
         dr, dc = SIDES[i]
         if dc == 0:
-            side = 0 if dr < 0 else 1
-            source, target = send_row.at[side], got_row.at[1 - side, pl.ds(8, tile_rows), :]
+            source = send_row.at[0 if dr < 0 else 1]
         elif dr == 0:
-            side = 0 if dc < 0 else 1
-            source, target = send_col.at[side], got_col.at[1 - side]
+            source = send_col.at[0 if dc < 0 else 1]
         else:
-            lanes = pl.ds(0 if dc < 0 else (panels - 1) * LANES, LANES)
-            corner = (2 if dr < 0 else 0) + (1 if dc < 0 else 0)
-            source, target = edge.at[0 if dr < 0 else 1, :, lanes], got_corner.at[corner]
+            source = edge.at[0 if dr < 0 else 1, :, pl.ds(0 if dc < 0 else (panels - 1) * LANES, LANES)]
         return pltpu.make_async_remote_copy(
-            src_ref=source, dst_ref=target, send_sem=send_sem.at[i], recv_sem=recv_sem.at[i],
+            src_ref=source, dst_ref=landing(i), send_sem=send_sem.at[i], recv_sem=recv_sem.at[i],
             device_id=(row + dr, cols_at + dc), device_id_type=MESH,
         )
 
-    for i, (dr, dc) in enumerate(SIDES):
-        @pl.when(there(dr, dc))
-        def _(i=i):
-            remote(i).start()
+    def send():
+        pl.semaphore_wait(barrier, count)
+        for i, (dr, dc) in enumerate(SIDES):
+            @pl.when(there(dr, dc))
+            def _(i=i):
+                remote(i).start()
 
     at16 = iota((16, LANES), 1)
     in16 = iota((16, LANES), 0)
@@ -282,6 +283,7 @@
         return 0
 
     lax.fori_loop(2, panels, next_panel, 0)
+    pl.when(jnp.logical_not(distant))(send)
 
     at_rows = iota((rows, LANES), 1)
     next_lanes = at_rows < LANES // 2
@@ -298,8 +300,9 @@
         lhs = jnp.concatenate([hi, lo, hi, edges], axis=1)
         rhs = jnp.concatenate([whi[p - 1], whi[p - 1], wlo[p - 1]], axis=0)
         both = jnp.dot(lhs, rhs, preferred_element_type=F32)
-        u_ref[p - 1] = both[:, :LANES]
-        w_ref[...] = both[:, LANES:]
+        w_ref[...] = both
+        u_edge[p - 1, 0:16, :] = both[0:16, :LANES]
+        u_edge[p - 1, 16:32, :] = both[rows - 16 :, :LANES]
 
     def own_rows(p, w_ref):
         for g in range(groups):
@@ -309,15 +312,31 @@
             o_sum = vx[p, pl.ds(at - 1, 8, stride=2), :] + vx[p, pl.ds(at + 3, 8, stride=2), :]
             c = [half[n, 8 * g : 8 * g + 8, :] for n in range(4)]
             ge[p - 1, PAD + 8 * g : PAD + 8 * g + 8, :] = (
-                e + w_ref[16 * g : 16 * g + 8, :] + ((c[0] * e + c[2] * o) + (0.5 * d0) * e_sum)
+                e + w_ref[16 * g : 16 * g + 8, LANES:] + ((c[0] * e + c[2] * o) + (0.5 * d0) * e_sum)
             )
             go[p - 1, PAD + 8 * g : PAD + 8 * g + 8, :] = (
-                o + w_ref[16 * g + 8 : 16 * g + 16, :] + ((c[1] * o + c[3] * e) + (0.5 * d1) * o_sum)
+                o + w_ref[16 * g + 8 : 16 * g + 16, LANES:] + ((c[1] * o + c[3] * e) + (0.5 * d1) * o_sum)
             )
+        for g in range(1, groups - 1):
+            at = PAD + 8 * g
+            e, o = ge[p - 1, at : at + 8, :], go[p - 1, at : at + 8, :]
+            e_sum = ge[p - 1, at - 1 : at + 7, :] + ge[p - 1, at + 1 : at + 9, :]
+            o_sum = go[p - 1, at - 1 : at + 7, :] + go[p - 1, at + 1 : at + 9, :]
+            c = [full[n, 8 * g : 8 * g + 8, :] for n in range(4)]
+            stage[p - 1, pl.ds(16 * g, 8, stride=2), :] = (
+                w_ref[16 * g : 16 * g + 8, :LANES] + ((c[0] * e + c[2] * o) + d0 * e_sum)
+            )
+            stage[p - 1, pl.ds(16 * g + 1, 8, stride=2), :] = (
+                w_ref[16 * g + 8 : 16 * g + 16, :LANES] + ((c[1] * o + c[3] * e) + d1 * o_sum)
+            )
 
     columns(2, w_one)
 
+    steps = (panels - 4) // 2
+    early = 1
+
     def middle(i, _):
+        pl.when(distant & (i == early))(send)
         p = 3 + 2 * i
         own_rows(p - 1, w_one)
         columns(p, w_two)
@@ -325,7 +344,7 @@
         columns(p + 1, w_one)
         return 0
 
-    lax.fori_loop(0, (panels - 4) // 2, middle, 0)
+    lax.fori_loop(0, steps, middle, 0)
     own_rows(panels - 2, w_one)
     columns(panels - 1, w_two)
 
@@ -349,24 +368,61 @@
     columns(panels, w_two)
     own_rows(panels, w_two)
 
-    for dr, dc in SIDES:
-        if dr:
-            wait_recv(dr, dc)
-    for side in (0, 1):
-        left, right = got_corner[2 * side], got_corner[2 * side + 1]
-        if side == 0:
-            tile_g[0:8, :] = right
-            got_row[side, 0:8, :] = left
-            got_row[side, 8 + tile_rows : 16 + tile_rows, :] = tile_g[4:12, :]
-        else:
-            tile_g[8:16, :] = left
-            got_row[side, 0:8, :] = tile_g[4:12, :]
-            got_row[side, 8 + tile_rows : 16 + tile_rows, :] = right
-    even8 = lane8 % 2 == 0
+    per_panel = LANES // 16
+    even_lane = lane8 % 2 == 0
+
+    def add_noise(g, t, move):
+        c = [col[i, pl.ds(t, 1), :] for i in (0, 1, 2, 10, 11)]
+        here = slice(8 * g, 8 * g + 8)
+        f = [full[i, here, :] for i in range(4)]
+        n_e, n_o, n_x = (noise[i, here, :] for i in range(3))
+        gap = (move * (LANES // 2) + lane8 // 2) - (8 * (g % per_panel) + sub8)
+        on, beside = gap == 0, jnp.abs(gap) == 1
+        for odd, s_r, x_r, d_r, one, two, mine, mate in (
+            (0, f[0], f[2], d0, c[3], c[4], jnp.where(even_lane, n_e, n_x), jnp.where(even_lane, n_x, n_e)),
+            (1, f[1], f[3], d1, c[4], c[3], jnp.where(even_lane, n_x, n_o), jnp.where(even_lane, n_o, n_x)),
+        ):
+            centre = mine + 0.5 * ((s_r * one + x_r * two) + (c[0] * mine + c[1] * mate))
+            side = 0.5 * (d_r * one + c[2] * mine)
+            value = jnp.where(on, centre, jnp.where(beside, side, 0.0))
+            if g in (0, groups - 1):
+                at = 8 * odd + (16 if g else 0)
+                u_edge[t, at : at + 8, :] += value
+            else:
+                stage[t, pl.ds(16 * g + odd, 8, stride=2), :] += value
+
+    ratio = panels * LANES // rows
+    first_panel = (row - cols_at * ratio) * (rows // LANES)
+
+    @pl.when((first_panel >= 0) & (first_panel < panels))
+    def _():
+        for g in range(groups):
+            t = first_panel + g // per_panel
+            add_noise(g, t, 0)
+            if g % per_panel == 0 and g:
+                add_noise(g, t - 1, -1)
+            if g % per_panel == per_panel - 1 and g < groups - 1:
+                add_noise(g, t + 1, 1)
+
+    @pl.when((first_panel >= 1) & (first_panel <= panels))
+    def _():
+        add_noise(0, first_panel - 1, -1)
+
+    @pl.when((first_panel + rows // LANES >= 0) & (first_panel + rows // LANES < panels))
+    def _():
+        add_noise(groups - 1, first_panel + rows // LANES, 1)
+
     upper = sub8 < 4
     species = sub8 % 2 == 0
+    for k in range(panels // 2):
+        here = slice(8 * k, 8 * k + 8)
+        one, two = 2 * k + 1, 2 * k + 2
+        e = PAD + rows
+        inner[0, here, :] = jnp.where(upper, vx[one, PAD - 2 : PAD + 6, :], vx[two, PAD - 6 : PAD + 2, :])
+        inner[1, here, :] = jnp.where(upper, vx[one, e - 2 : e + 6, :], vx[two, e - 6 : e + 2, :])
+        for i in range(3):
+            halo_col[i, here, :] = jnp.where(upper, col[i, 2 * k : 2 * k + 1, :], col[i, 2 * k + 1 : 2 * k + 2, :])
     for side in (0, 1):
-        ok = there(-1, 0) if side == 0 else there(1, 0)
         voxel = jnp.clip(row * half_rows + (-1 if side == 0 else half_rows), 0, voxels - 1)
         pick = lane8 * 0 + voxel % LANES
         a = jnp.broadcast_to(feed_of[pl.ds(voxel // LANES, 1), :], (8, LANES))
@@ -376,80 +432,20 @@
         end = (voxel == 0) | (voxel == voxels - 1)
         near = jnp.where(end, 1.0, 2.0)
         d_r = jnp.where(species, d0, d1)
-        s_r = STEP * jnp.where(species, b - 1.0, -a * a) - d_r * near
-        x_r = STEP * jnp.where(species, a * a, -b)
-        for k in range(panels // 2):
-            at = 8 + 8 * k
-            one, two = 2 * k + 1, 2 * k + 2
-            tile, left, right = (got_row[side, at + t : at + t + 8, :] for t in (0, -4, 4))
-            c_s, c_x, c_d = (
-                jnp.where(upper, col[i, 2 * k : 2 * k + 1, :], col[i, 2 * k + 1 : 2 * k + 2, :]) for i in range(3)
-            )
-            mate = jnp.where(even8, pltpu.roll(tile, LANES - 1, 1), pltpu.roll(tile, 1, 1))
-            far = pltpu.roll(jnp.where(lane8 >= LANES - 2, left, tile), 2, 1) + pltpu.roll(
-                jnp.where(lane8 < 2, right, tile), LANES - 2, 1
-            )
-            w = c_s * tile + c_x * mate + c_d * far
-            row_mate = jnp.where(species, got_row[side, at + 1 : at + 9, :], got_row[side, at - 1 : at + 7, :])
-            if side == 0:
-                out = got_row[side, at - 2 : at + 6, :]
-                inn = jnp.where(upper, vx[one, PAD - 2 : PAD + 6, :], vx[two, PAD - 6 : PAD + 2, :])
-            else:
-                out = got_row[side, at + 2 : at + 10, :]
-                e = PAD + rows
-                inn = jnp.where(upper, vx[one, e - 2 : e + 6, :], vx[two, e - 6 : e + 2, :])
-            g = tile + w + 0.5 * (s_r * tile + x_r * row_mate + d_r * (out + inn))
-            tile_g[8 + 8 * k : 16 + 8 * k, :] = jnp.where(ok, g, 0.0)
-        for k in range(panels // 2):
-            for t in (0, 1):
-                p, at = 2 * k + t, 8 + 8 * k + 4 * t
-                for ref, o, dd in ((ge, 0, d0), (go, 1, d1)):
-                    if side == 0:
-                        ref[p, 0:8, :] = tile_g[at + 2 + o - 7 : at + 2 + o + 1, :]
-                        here, sub, from_ = slice(PAD, PAD + 8), 0, at + 2 + o
-                    else:
-                        end = PAD + half_rows
-                        ref[p, end : end + 8, :] = tile_g[at + o : at + o + 8, :]
-                        here, sub, from_ = slice(end - 8, end), 7, at + o - 7
-                    ref[p, here, :] += jnp.where(sub8 == sub, (0.5 * dd) * got_row[side, from_ : from_ + 8, :], 0.0)
-
-    per_panel = LANES // 16
-
-    def add_noise(g, t, move):
-        c = [col[i, pl.ds(t, 1), :] for i in (0, 1, 2, 10, 11)]
-        here = slice(8 * g, 8 * g + 8)
-        f = [full[i, here, :] for i in range(4)]
-        n_e, n_o, n_x = (noise[i, here, :] for i in range(3))
-        gap = (move * (LANES // 2) + lane8 // 2) - (8 * (g % per_panel) + sub8)
-        on, beside = gap == 0, jnp.abs(gap) == 1
-        for start, s_r, x_r, d_r, one, two, mine, mate in (
-            (16 * g, f[0], f[2], d0, c[3], c[4], jnp.where(even8, n_e, n_x), jnp.where(even8, n_x, n_e)),
-            (16 * g + 8, f[1], f[3], d1, c[4], c[3], jnp.where(even8, n_x, n_o), jnp.where(even8, n_o, n_x)),
-        ):
-            centre = mine + 0.5 * ((s_r * one + x_r * two) + (c[0] * mine + c[1] * mate))
-            side = 0.5 * (d_r * one + c[2] * mine)
-            u_ref[t, start : start + 8, :] += jnp.where(on, centre, jnp.where(beside, side, 0.0))
-
-    ratio = panels * LANES // rows
-    first_panel = (row - cols_at * ratio) * (rows // LANES)
-
-    @pl.when((first_panel >= 0) & (first_panel < panels))
-    def _():
-        for g in range(groups):
-            t = first_panel + g // per_panel
-            add_noise(g, t, 0)
-            if g % per_panel == 0 and g:
-                add_noise(g, t - 1, -1)
-            if g % per_panel == per_panel - 1 and g < groups - 1:
-                add_noise(g, t + 1, 1)
-
-    @pl.when((first_panel >= 1) & (first_panel <= panels))
-    def _():
-        add_noise(0, first_panel - 1, -1)
-
-    @pl.when((first_panel + rows // LANES >= 0) & (first_panel + rows // LANES < panels))
-    def _():
-        add_noise(groups - 1, first_panel + rows // LANES, 1)
+        halo_row[side, 0] = jnp.broadcast_to(STEP * jnp.where(species, b - 1.0, -a * a) - d_r * near, (8, LANES))
+        halo_row[side, 1] = jnp.broadcast_to(STEP * jnp.where(species, a * a, -b), (8, LANES))
+        halo_row[side, 2] = jnp.broadcast_to(d_r, (8, LANES))
+        ok = there(-1, 0) if side == 0 else there(1, 0)
+        halo_row[side, 3] = jnp.full((8, LANES), ok.astype(F32))
+
+    for dr, dc in SIDES:
+        if dr:
+            wait_recv(dr, dc)
+    for side in (0, 1):
+        halo[side, 8 : 8 + tile_rows, :] = got_row[side, 8 : 8 + tile_rows, :]
+        halo[side, 0:8, :] = got_corner[2 * side] if side == 0 else pltpu.roll(got_corner[2 * side], 4, 0)
+        right = got_corner[2 * side + 1]
+        halo[side, 8 + tile_rows : 16 + tile_rows, :] = pltpu.roll(right, 4, 0) if side == 0 else right
 
     for i, (dr, dc) in enumerate(SIDES):
         @pl.when(there(dr, dc))
@@ -457,39 +453,80 @@
             remote(i).wait_send()
 
 
-def finish_kernel(rows, panels, u_ref, ge, go, full, spread, out, stage, sem):
+def finish_kernel(
+    rows, panels,
+    stage, u_edge, ge, go, full, spread, halo, inner, halo_col, halo_row,
+    out, tile_g, near_g, ends, wide, sem,
+):
     d0, d1 = spread[0], spread[1]
     groups = rows // 16
-    wide = 4
+    half_rows = rows // 2
 
     def store(p):
         return pltpu.make_async_copy(
-            stage.at[p], out.at[:, pl.ds(pl.multiple_of(p * LANES, LANES), LANES)], sem.at[p]
+            stage.at[p, pl.ds(16, rows - 32), :],
+            out.at[pl.ds(16, rows - 32), pl.ds(p * LANES, LANES)],
+            sem.at[p],
         )
 
-    def step(n, _):
-        for g in range(groups):
-            c = [full[i, 8 * g : 8 * g + 8, :] for i in range(4)]
-            for t in range(wide):
-                p = n * wide + t
-                at = PAD + 8 * g
-                e, o = ge[p, at : at + 8, :], go[p, at : at + 8, :]
-                e_sum = ge[p, at - 1 : at + 7, :] + ge[p, at + 1 : at + 9, :]
-                o_sum = go[p, at - 1 : at + 7, :] + go[p, at + 1 : at + 9, :]
-                u_e, u_o = u_ref[p, 16 * g : 16 * g + 8, :], u_ref[p, 16 * g + 8 : 16 * g + 16, :]
-                stage[p, pl.ds(16 * g, 8, stride=2), :] = u_e + ((c[0] * e + c[2] * o) + d0 * e_sum)
-                stage[p, pl.ds(16 * g + 1, 8, stride=2), :] = u_o + ((c[1] * o + c[3] * e) + d1 * o_sum)
-        for t in range(wide):
-            store(n * wide + t).start()
-        return 0
-
-    lax.fori_loop(0, panels // wide, step, 0)
-
-    def drain(p, _):
+    def store_end(side):
+        return pltpu.make_async_copy(
+            wide.at[side], out.at[pl.ds(side * (rows - 16), 16), :], sem.at[panels + side]
+        )
+
+    for p in range(panels):
+        store(p).start()
+
+    lane8 = iota((8, LANES), 1)
+    sub8 = iota((8, LANES), 0)
+    even8 = lane8 % 2 == 0
+    species = sub8 % 2 == 0
+    for side in (0, 1):
+        s_r, x_r, d_r = halo_row[side, 0], halo_row[side, 1], halo_row[side, 2]
+        ok = halo_row[side, 3] > 0.5
+        for k in range(panels // 2):
+            at = 8 + 8 * k
+            here = slice(8 * k, 8 * k + 8)
+            tile, left, right = (halo[side, at + t : at + t + 8, :] for t in (0, -4, 4))
+            mate = jnp.where(even8, pltpu.roll(tile, LANES - 1, 1), pltpu.roll(tile, 1, 1))
+            beside = pltpu.roll(jnp.where(lane8 >= LANES - 2, left, tile), 2, 1) + pltpu.roll(
+                jnp.where(lane8 < 2, right, tile), LANES - 2, 1
+            )
+            w = halo_col[0, here, :] * tile + halo_col[1, here, :] * mate + halo_col[2, here, :] * beside
+            row_mate = jnp.where(species, halo[side, at + 1 : at + 9, :], halo[side, at - 1 : at + 7, :])
+            away = halo[side, at - 2 : at + 6, :] if side == 0 else halo[side, at + 2 : at + 10, :]
+            g = tile + w + 0.5 * (s_r * tile + x_r * row_mate + d_r * (away + inner[side, here, :]))
+            tile_g[side, at : at + 8, :] = jnp.where(ok, g, 0.0)
+
+        first = 0 if side == 0 else half_rows - 8
+        c = [full[i, first : first + 8, :] for i in range(4)]
+        for p in range(panels):
+            at = 8 + 8 * (p // 2) + 4 * (p % 2)
+            for o, ref, dd in ((0, ge, d0), (1, go, d1)):
+                mine = ref[p, PAD + first : PAD + first + 8, :]
+                if side == 0:
+                    fix = halo[side, at + 2 + o : at + 10 + o, :]
+                    near_g[o, 0:8, :] = tile_g[side, at + o - 5 : at + o + 3, :]
+                    near_g[o, 16:24, :] = ref[p, PAD + 8 : PAD + 16, :]
+                else:
+                    fix = halo[side, at + o - 7 : at + o + 1, :]
+                    near_g[o, 0:8, :] = ref[p, PAD + first - 8 : PAD + first, :]
+                    near_g[o, 16:24, :] = tile_g[side, at + o : at + o + 8, :]
+                fix = jnp.where(ok & (sub8 == (0 if side == 0 else 7)), (0.5 * dd) * fix, 0.0)
+                near_g[o, 8:16, :] = mine + fix
+            e, o = near_g[0, 8:16, :], near_g[1, 8:16, :]
+            e_sum = near_g[0, 7:15, :] + near_g[0, 9:17, :]
+            o_sum = near_g[1, 7:15, :] + near_g[1, 9:17, :]
+            u = 16 * side
+            ends[p, pl.ds(0, 8, stride=2), :] = u_edge[p, u : u + 8, :] + ((c[0] * e + c[2] * o) + d0 * e_sum)
+            ends[p, pl.ds(1, 8, stride=2), :] = u_edge[p, u + 8 : u + 16, :] + ((c[1] * o + c[3] * e) + d1 * o_sum)
+            wide[side, :, LANES * p : LANES * p + LANES] = ends[p]
+        store_end(side).start()
+
+    for p in range(panels):
         store(p).wait()
-        return 0
-
-    lax.fori_loop(0, panels, drain, 0)
+    for side in (0, 1):
+        store_end(side).wait()
 
 
 def body(covariance, classes, feed_rate, conversion_rate, diffusion):
@@ -505,21 +542,26 @@
         functools.partial(advance_kernel, rows, panels, voxels, *sizes),
         out_shape=[
             pltpu.VMEM((panels, rows, LANES), F32),
+            pltpu.VMEM((panels, 32, LANES), F32),
             pltpu.VMEM((panels, half_rows + 2 * PAD, LANES), F32),
             pltpu.VMEM((panels, half_rows + 2 * PAD, LANES), F32),
             pltpu.VMEM((4, half_rows, LANES), F32),
             pltpu.VMEM((2, 8, LANES), F32),
+            pltpu.VMEM((2, 4 * panels + 16, LANES), F32),
+            pltpu.VMEM((2, 4 * panels, LANES), F32),
+            pltpu.VMEM((3, 4 * panels, LANES), F32),
+            pltpu.VMEM((2, 4, 8, LANES), F32),
         ],
         in_specs=[hbm] * 5,
-        out_specs=[vmem] * 5,
+        out_specs=[vmem] * 10,
         scratch_shapes=[
             pltpu.VMEM((panels + 2, rows + 2 * PAD, LANES), F32),
             pltpu.VMEM((panels + 2, rows, LANES), BF16),
             pltpu.VMEM((panels + 2, rows, LANES), BF16),
             pltpu.VMEM((panels, LANES, 2 * LANES), BF16),
             pltpu.VMEM((panels, 2 * LANES, 2 * LANES), BF16),
-            pltpu.VMEM((rows, LANES), F32),
-            pltpu.VMEM((rows, LANES), F32),
+            pltpu.VMEM((rows, 2 * LANES), F32),
+            pltpu.VMEM((rows, 2 * LANES), F32),
             pltpu.VMEM((4, half_rows, LANES), F32),
             pltpu.VMEM((3, half_rows, LANES), F32),
             pltpu.VMEM((voxels // LANES, LANES), F32),
@@ -539,7 +581,6 @@
             pltpu.VMEM((2, 4 * panels + 16, LANES), F32),
             pltpu.VMEM((2, 16, LANES), F32),
             pltpu.VMEM((4, 8, LANES), F32),
-            pltpu.VMEM((4 * panels + 16, LANES), F32),
             pltpu.SemaphoreType.DMA((panels,)),
             pltpu.SemaphoreType.DMA((6,)),
             pltpu.SemaphoreType.DMA((8,)),
@@ -553,11 +594,14 @@
     return pl.pallas_call(
         functools.partial(finish_kernel, rows, panels),
         out_shape=jax.ShapeDtypeStruct((rows, cols), F32),
-        in_specs=[vmem] * 5,
+        in_specs=[vmem] * 10,
         out_specs=hbm,
         scratch_shapes=[
-            pltpu.VMEM((panels, rows, LANES), F32),
-            pltpu.SemaphoreType.DMA((panels,)),
+            pltpu.VMEM((2, 4 * panels + 16, LANES), F32),
+            pltpu.VMEM((2, 24, LANES), F32),
+            pltpu.VMEM((panels, 16, LANES), F32),
+            pltpu.VMEM((2, 16, cols), F32),
+            pltpu.SemaphoreType.DMA((panels + 2,)),
         ],
         compiler_params=pltpu.CompilerParams(vmem_limit_bytes=24 << 20),
         name="rows",

time: 16.1 us -> 15.5 us (0.963); the launches traced: 16 us -> 15.2 us
  Pallas kernels: 16 us -> 15.2 us
    pallas_call x1, Pallas kernels: 13.6 us -> 13 us  [body(): pl.pallas_call(functools.partial(advance_kernel, rows, panels, voxels, *s...]
    pallas_call x1, Pallas kernels: 2.43 us -> 2.22 us  [body(): pl.pallas_call(functools.partial(finish_kernel, rows, panels), out_shape=...]
where the time goes in v3:
time: 15.5 us; the launch traced here: 15.2 us
  Pallas kernels  15.2 us (98%)
    pallas_call x1, Pallas kernels, body(): pl.pallas_call(functools.partial(advance_kernel, rows, panels, voxels, *s...  13 us
    pallas_call x1, Pallas kernels, body(): pl.pallas_call(functools.partial(finish_kernel, rows, panels), out_shape=...  2.22 us

profile of v3, /device:TPU:63, one launch (start us, length us, event | category | flops | bytes accessed | tf_op | source)
XLA Modules:
  0.0 15.2 jit_solution(13300270718098227245)
XLA Ops:
  0.0 13.0 %halo_and_columns.1 = (f32[16,512,128]{2,1,0:T(8,128)S(1)}, f32[16,32,128]{2,1,0:T(8,128)S(1)}, f32[16,272,128]{2,1,0:T(8,128)S(1)}, f32[16,272,128]{2,1,0:T(8,1...) custom-call(f32[512,2048]{1,0:T(8,128)} %cov.1, ...), custom_call_target="tpu_custom_call" | custom-call | tf_op jit(solution)/shard_map/halo_and_columns/pallas_call | solution.py:541
  13.0 2.2 %rows.1 = f32[512,2048]{1,0:T(8,128)} custom-call(f32[16,512,128]{2,1,0:T(8,128)S(1)} %get-tuple-element.15.stage, f32[16,32,128]{2,1,0:T(8,128)S(1)} %get-tuple-element.16.u_edge, f32[16,272,128]{2,1,0:T(8,128)S(1)} %get-tuple-element.17.ge, f32[16,272,128]{2,1,0:T(8,128)S(1)} %get-tuple-element.18.go, f32[4,256,128]{2,1,0:T(8,128)S(1)} %get-tuple-element.19.full, ...), custom_call_target="tpu_custom_call" | custom-call | tf_op jit(solution)/shard_map/rows/pallas_call | solution.py:594

commit v4 on v3

--- a/solution.py
+++ b/solution.py
@@ -45,15 +45,24 @@
 
     barrier = pltpu.get_barrier_semaphore()
     count = jnp.int32(0)
+    across = {1: row == grid_rows // 2 - 1, -1: row == grid_rows // 2}
+    distant = across[1] | across[-1]
+
+    def each_side(act):
+        for dr in (1, -1):
+            @pl.when(across[dr])
+            def _(dr=dr):
+                for dc in (0, 1, -1):
+                    pl.when(there(dr, dc))(lambda dc=dc: act(dr, dc))
+        for dr, dc in SIDES:
+            ok = there(dr, dc)
+            pl.when(ok & jnp.logical_not(across[dr]) if dr else ok)(lambda dr=dr, dc=dc: act(dr, dc))
+
     for dr, dc in SIDES:
-        ok = there(dr, dc)
-        count += ok.astype(jnp.int32)
-
-        @pl.when(ok)
-        def _(dr=dr, dc=dc):
-            pl.semaphore_signal(barrier, inc=1, device_id=(row + dr, cols_at + dc), device_id_type=MESH)
-
-    distant = (row == grid_rows // 2 - 1) | (row == grid_rows // 2)
+        count += there(dr, dc).astype(jnp.int32)
+    each_side(lambda dr, dc: pl.semaphore_signal(
+        barrier, inc=1, device_id=(row + dr, cols_at + dc), device_id_type=MESH
+    ))
 
     small = [
         pltpu.make_async_copy(a, b, small_sem.at[n])
@@ -224,10 +233,7 @@
 
     def send():
         pl.semaphore_wait(barrier, count)
-        for i, (dr, dc) in enumerate(SIDES):
-            @pl.when(there(dr, dc))
-            def _(i=i):
-                remote(i).start()
+        each_side(lambda dr, dc: remote(SIDES.index((dr, dc))).start())
 
     at16 = iota((16, LANES), 1)
     in16 = iota((16, LANES), 0)
@@ -283,7 +289,8 @@
         return 0
 
     lax.fori_loop(2, panels, next_panel, 0)
-    pl.when(jnp.logical_not(distant))(send)
+    odd = cols_at % 2 == 1
+    pl.when(jnp.logical_not(distant | odd))(send)
 
     at_rows = iota((rows, LANES), 1)
     next_lanes = at_rows < LANES // 2
@@ -336,7 +343,7 @@
     early = 1
 
     def middle(i, _):
-        pl.when(distant & (i == early))(send)
+        pl.when((distant | odd) & (i == early))(send)
         p = 3 + 2 * i
         own_rows(p - 1, w_one)
         columns(p, w_two)

time: 15.5 us -> 15.7 us (1.013)
  Pallas kernels: 15.2 us -> 15.6 us
    pallas_call x1, Pallas kernels: 13 us -> 13.4 us  [body(): pl.pallas_call(functools.partial(advance_kernel, rows, panels, voxels, *s...]
where the time goes in v4:
time: 15.7 us; the launch traced here: 15.6 us
  Pallas kernels  15.6 us (99%)
    pallas_call x1, Pallas kernels, body(): pl.pallas_call(functools.partial(advance_kernel, rows, panels, voxels, *s...  13.4 us
    pallas_call x1, Pallas kernels, body(): pl.pallas_call(functools.partial(finish_kernel, rows, panels), out_shape=...  2.22 us

profile of v4, /device:TPU:63, one launch (start us, length us, event | category | flops | bytes accessed | tf_op | source)
XLA Modules:
  0.0 15.6 jit_solution(1926291289302574257)
XLA Ops:
  0.0 13.4 %halo_and_columns.1 = (f32[16,512,128]{2,1,0:T(8,128)S(1)}, f32[16,32,128]{2,1,0:T(8,128)S(1)}, f32[16,272,128]{2,1,0:T(8,128)S(1)}, f32[16,272,128]{2,1,0:T(8,1...) custom-call(f32[512,2048]{1,0:T(8,128)} %cov.1, ...), custom_call_target="tpu_custom_call" | custom-call | tf_op jit(solution)/shard_map/halo_and_columns/pallas_call | solution.py:548
  13.4 2.2 %rows.1 = f32[512,2048]{1,0:T(8,128)} custom-call(f32[16,512,128]{2,1,0:T(8,128)S(1)} %get-tuple-element.15.stage, f32[16,32,128]{2,1,0:T(8,128)S(1)} %get-tuple-element.16.u_edge, f32[16,272,128]{2,1,0:T(8,128)S(1)} %get-tuple-element.17.ge, f32[16,272,128]{2,1,0:T(8,128)S(1)} %get-tuple-element.18.go, f32[4,256,128]{2,1,0:T(8,128)S(1)} %get-tuple-element.19.full, ...), custom_call_target="tpu_custom_call" | custom-call | tf_op jit(solution)/shard_map/rows/pallas_call | solution.py:601

commit v5 on v4

--- a/solution.py
+++ b/solution.py
@@ -27,9 +27,9 @@
 def advance_kernel(
     rows, panels, voxels, grid_rows, grid_cols,
     cov, classes_in, feed_in, conv_in, diff_in,
-    stage, u_edge, ge, go, full, spread, halo, inner, halo_col, halo_row,
+    stage, u_edge, ge, go, full, spread, got_row, got_corner, inner, halo_col, halo_row,
     vx, high, low, whi, wlo, w_one, w_two, half, noise, feed_of, conv_of, ext_s, ext_x, ext_a, ext_b, col,
-    classes, feed, conv, diff, edge, send_row, send_col, got_row, got_col, got_corner,
+    classes, feed, conv, diff, edge, send_row, send_col, got_col,
     load_sem, small_sem, send_sem, recv_sem,
 ):
     row, cols_at = lax.axis_index("row"), lax.axis_index("col")
@@ -52,7 +52,7 @@
         for dr in (1, -1):
             @pl.when(across[dr])
             def _(dr=dr):
-                for dc in (0, 1, -1):
+                for dc in (-1, 0, 1):
                     pl.when(there(dr, dc))(lambda dc=dc: act(dr, dc))
         for dr, dc in SIDES:
             ok = there(dr, dc)
@@ -213,7 +213,7 @@
     def landing(i):
         dr, dc = SIDES[i]
         if dc == 0:
-            return got_row.at[0 if dr > 0 else 1, pl.ds(8, tile_rows), :]
+            return got_row.at[0 if dr > 0 else 1]
         if dr == 0:
             return got_col.at[0 if dc > 0 else 1]
         return got_corner.at[(2 if dr < 0 else 0) + (1 if dc < 0 else 0)]
@@ -445,25 +445,20 @@
         ok = there(-1, 0) if side == 0 else there(1, 0)
         halo_row[side, 3] = jnp.full((8, LANES), ok.astype(F32))
 
-    for dr, dc in SIDES:
-        if dr:
-            wait_recv(dr, dc)
-    for side in (0, 1):
-        halo[side, 8 : 8 + tile_rows, :] = got_row[side, 8 : 8 + tile_rows, :]
-        halo[side, 0:8, :] = got_corner[2 * side] if side == 0 else pltpu.roll(got_corner[2 * side], 4, 0)
-        right = got_corner[2 * side + 1]
-        halo[side, 8 + tile_rows : 16 + tile_rows, :] = pltpu.roll(right, 4, 0) if side == 0 else right
-
     for i, (dr, dc) in enumerate(SIDES):
         @pl.when(there(dr, dc))
         def _(i=i):
             remote(i).wait_send()
 
+    for dr, dc in SIDES:
+        if dr:
+            wait_recv(dr, dc)
+
 
 def finish_kernel(
     rows, panels,
-    stage, u_edge, ge, go, full, spread, halo, inner, halo_col, halo_row,
-    out, tile_g, near_g, ends, wide, sem,
+    stage, u_edge, ge, go, full, spread, got_row, got_corner, inner, halo_col, halo_row,
+    out, halo, tile_g, near_g, ends, wide, sem,
 ):
     d0, d1 = spread[0], spread[1]
     groups = rows // 16
@@ -483,6 +478,13 @@
 
     for p in range(panels):
         store(p).start()
+
+    tile_rows = 4 * panels
+    for side in (0, 1):
+        left, right = got_corner[2 * side], got_corner[2 * side + 1]
+        halo[side, 8 : 8 + tile_rows, :] = got_row[side]
+        halo[side, 0:8, :] = left if side == 0 else pltpu.roll(left, 4, 0)
+        halo[side, 8 + tile_rows : 16 + tile_rows, :] = pltpu.roll(right, 4, 0) if side == 0 else right
 
     lane8 = iota((8, LANES), 1)
     sub8 = iota((8, LANES), 0)
@@ -554,13 +556,14 @@
             pltpu.VMEM((panels, half_rows + 2 * PAD, LANES), F32),
             pltpu.VMEM((4, half_rows, LANES), F32),
             pltpu.VMEM((2, 8, LANES), F32),
-            pltpu.VMEM((2, 4 * panels + 16, LANES), F32),
+            pltpu.VMEM((2, 4 * panels, LANES), F32),
+            pltpu.VMEM((4, 8, LANES), F32),
             pltpu.VMEM((2, 4 * panels, LANES), F32),
             pltpu.VMEM((3, 4 * panels, LANES), F32),
             pltpu.VMEM((2, 4, 8, LANES), F32),
         ],
         in_specs=[hbm] * 5,
-        out_specs=[vmem] * 10,
+        out_specs=[vmem] * 11,
         scratch_shapes=[
             pltpu.VMEM((panels + 2, rows + 2 * PAD, LANES), F32),
             pltpu.VMEM((panels + 2, rows, LANES), BF16),
@@ -585,9 +588,7 @@
             pltpu.VMEM((2, 8, cols), F32),
             pltpu.VMEM((2, 4 * panels, LANES), F32),
             pltpu.VMEM((2, 16, LANES), F32),
-            pltpu.VMEM((2, 4 * panels + 16, LANES), F32),
             pltpu.VMEM((2, 16, LANES), F32),
-            pltpu.VMEM((4, 8, LANES), F32),
             pltpu.SemaphoreType.DMA((panels,)),
             pltpu.SemaphoreType.DMA((6,)),
             pltpu.SemaphoreType.DMA((8,)),
@@ -601,9 +602,10 @@
     return pl.pallas_call(
         functools.partial(finish_kernel, rows, panels),
         out_shape=jax.ShapeDtypeStruct((rows, cols), F32),
-        in_specs=[vmem] * 10,
+        in_specs=[vmem] * 11,
         out_specs=hbm,
         scratch_shapes=[
+            pltpu.VMEM((2, 4 * panels + 16, LANES), F32),
             pltpu.VMEM((2, 4 * panels + 16, LANES), F32),
             pltpu.VMEM((2, 24, LANES), F32),
             pltpu.VMEM((panels, 16, LANES), F32),

time: 15.7 us -> 15.4 us (0.981)
  Pallas kernels: 15.6 us -> 15.2 us
    pallas_call x1, Pallas kernels: 13.4 us -> 13 us  [body(): pl.pallas_call(functools.partial(advance_kernel, rows, panels, voxels, *s...]
where the time goes in v5:
time: 15.4 us; the launch traced here: 15.2 us
  Pallas kernels  15.2 us (99%)
    pallas_call x1, Pallas kernels, body(): pl.pallas_call(functools.partial(advance_kernel, rows, panels, voxels, *s...  13 us
    pallas_call x1, Pallas kernels, body(): pl.pallas_call(functools.partial(finish_kernel, rows, panels), out_shape=...  2.22 us

profile of v5, /device:TPU:63, one launch (start us, length us, event | category | flops | bytes accessed | tf_op | source)
XLA Modules:
  0.0 15.2 jit_solution(3510720074168538441)
XLA Ops:
  0.0 13.0 %halo_and_columns.1 = (f32[16,512,128]{2,1,0:T(8,128)S(1)}, f32[16,32,128]{2,1,0:T(8,128)S(1)}, f32[16,272,128]{2,1,0:T(8,128)S(1)}, f32[16,272,128]{2,1,0:T(8,1...) custom-call(f32[512,2048]{1,0:T(8,128)} %cov.1, ...), custom_call_target="tpu_custom_call" | custom-call | tf_op jit(solution)/shard_map/halo_and_columns/pallas_call | solution.py:550
  13.0 2.2 %rows.1 = f32[512,2048]{1,0:T(8,128)} custom-call(f32[16,512,128]{2,1,0:T(8,128)S(1)} %get-tuple-element.16.stage, f32[16,32,128]{2,1,0:T(8,128)S(1)} %get-tuple-element.17.u_edge, f32[16,272,128]{2,1,0:T(8,128)S(1)} %get-tuple-element.18.ge, f32[16,272,128]{2,1,0:T(8,128)S(1)} %get-tuple-element.19.go, f32[4,256,128]{2,1,0:T(8,128)S(1)} %get-tuple-element.20.full, ...), custom_call_target="tpu_custom_call" | custom-call | tf_op jit(solution)/shard_map/rows/pallas_call | solution.py:602

commit v6 on v5

--- a/solution.py
+++ b/solution.py
@@ -529,7 +529,7 @@
             u = 16 * side
             ends[p, pl.ds(0, 8, stride=2), :] = u_edge[p, u : u + 8, :] + ((c[0] * e + c[2] * o) + d0 * e_sum)
             ends[p, pl.ds(1, 8, stride=2), :] = u_edge[p, u + 8 : u + 16, :] + ((c[1] * o + c[3] * e) + d1 * o_sum)
-            wide[side, :, LANES * p : LANES * p + LANES] = ends[p]
+            wide[side, :, LANES * p : LANES * p + LANES] = ends[p, 0:16, :]
         store_end(side).start()
 
     for p in range(panels):
@@ -608,7 +608,7 @@
             pltpu.VMEM((2, 4 * panels + 16, LANES), F32),
             pltpu.VMEM((2, 4 * panels + 16, LANES), F32),
             pltpu.VMEM((2, 24, LANES), F32),
-            pltpu.VMEM((panels, 16, LANES), F32),
+            pltpu.VMEM((panels, 24, LANES), F32),
             pltpu.VMEM((2, 16, cols), F32),
             pltpu.SemaphoreType.DMA((panels + 2,)),
         ],

time: 15.4 us -> 15.4 us (level)
  no operation moved by 1% of the time
where the time goes in v6:
time: 15.4 us; the launch traced here: 15.2 us
  Pallas kernels  15.2 us (99%)
    pallas_call x1, Pallas kernels, body(): pl.pallas_call(functools.partial(advance_kernel, rows, panels, voxels, *s...  13 us
    pallas_call x1, Pallas kernels, body(): pl.pallas_call(functools.partial(finish_kernel, rows, panels), out_shape=...  2.22 us

profile of v6, /device:TPU:63, one launch (start us, length us, event | category | flops | bytes accessed | tf_op | source)
XLA Modules:
  0.0 15.2 jit_solution(5842204941164036248)
XLA Ops:
  0.0 13.0 %halo_and_columns.1 = (f32[16,512,128]{2,1,0:T(8,128)S(1)}, f32[16,32,128]{2,1,0:T(8,128)S(1)}, f32[16,272,128]{2,1,0:T(8,128)S(1)}, f32[16,272,128]{2,1,0:T(8,1...) custom-call(f32[512,2048]{1,0:T(8,128)} %cov.1, ...), custom_call_target="tpu_custom_call" | custom-call | tf_op jit(solution)/shard_map/halo_and_columns/pallas_call | solution.py:550
  13.0 2.2 %rows.1 = f32[512,2048]{1,0:T(8,128)} custom-call(f32[16,512,128]{2,1,0:T(8,128)S(1)} %get-tuple-element.16.stage, f32[16,32,128]{2,1,0:T(8,128)S(1)} %get-tuple-element.17.u_edge, f32[16,272,128]{2,1,0:T(8,128)S(1)} %get-tuple-element.18.ge, f32[16,272,128]{2,1,0:T(8,128)S(1)} %get-tuple-element.19.go, f32[4,256,128]{2,1,0:T(8,128)S(1)} %get-tuple-element.20.full, ...), custom_call_target="tpu_custom_call" | custom-call | tf_op jit(solution)/shard_map/rows/pallas_call | solution.py:602

commit v7 on v6

--- a/solution.py
+++ b/solution.py
@@ -375,6 +375,12 @@
     columns(panels, w_two)
     own_rows(panels, w_two)
 
+    for dr in (1, -1):
+        @pl.when(jnp.logical_not(across[-dr]))
+        def _(dr=dr):
+            for dc in (0, 1, -1):
+                wait_recv(dr, dc)
+
     per_panel = LANES // 16
     even_lane = lane8 % 2 == 0
 
@@ -450,9 +456,11 @@
         def _(i=i):
             remote(i).wait_send()
 
-    for dr, dc in SIDES:
-        if dr:
-            wait_recv(dr, dc)
+    for dr in (1, -1):
+        @pl.when(across[-dr])
+        def _(dr=dr):
+            for dc in (0, 1, -1):
+                wait_recv(dr, dc)
 
 
 def finish_kernel(

time: 15.4 us -> 15.4 us (level)
  no operation moved by 1% of the time
where the time goes in v7:
time: 15.4 us; the launch traced here: 15.2 us
  Pallas kernels  15.2 us (99%)
    pallas_call x1, Pallas kernels, body(): pl.pallas_call(functools.partial(advance_kernel, rows, panels, voxels, *s...  13 us
    pallas_call x1, Pallas kernels, body(): pl.pallas_call(functools.partial(finish_kernel, rows, panels), out_shape=...  2.22 us

profile of v7, /device:TPU:63, one launch (start us, length us, event | category | flops | bytes accessed | tf_op | source)
XLA Modules:
  0.0 15.2 jit_solution(17698132174991376093)
XLA Ops:
  0.0 13.0 %halo_and_columns.1 = (f32[16,512,128]{2,1,0:T(8,128)S(1)}, f32[16,32,128]{2,1,0:T(8,128)S(1)}, f32[16,272,128]{2,1,0:T(8,128)S(1)}, f32[16,272,128]{2,1,0:T(8,1...) custom-call(f32[512,2048]{1,0:T(8,128)} %cov.1, ...), custom_call_target="tpu_custom_call" | custom-call | tf_op jit(solution)/shard_map/halo_and_columns/pallas_call | solution.py:558
  13.0 2.2 %rows.1 = f32[512,2048]{1,0:T(8,128)} custom-call(f32[16,512,128]{2,1,0:T(8,128)S(1)} %get-tuple-element.16.stage, f32[16,32,128]{2,1,0:T(8,128)S(1)} %get-tuple-element.17.u_edge, f32[16,272,128]{2,1,0:T(8,128)S(1)} %get-tuple-element.18.ge, f32[16,272,128]{2,1,0:T(8,128)S(1)} %get-tuple-element.19.go, f32[4,256,128]{2,1,0:T(8,128)S(1)} %get-tuple-element.20.full, ...), custom_call_target="tpu_custom_call" | custom-call | tf_op jit(solution)/shard_map/rows/pallas_call | solution.py:610

commit v8 on v6

--- a/solution.py
+++ b/solution.py
@@ -340,10 +340,11 @@
     columns(2, w_one)
 
     steps = (panels - 4) // 2
-    early = 1
+    place = cols_at // 2
+    turn = jnp.clip(jnp.where(across[1], 4 - place, jnp.where(across[-1], 1 + place, 1)), 0, steps - 1)
 
     def middle(i, _):
-        pl.when((distant | odd) & (i == early))(send)
+        pl.when((distant | odd) & (i == turn))(send)
         p = 3 + 2 * i
         own_rows(p - 1, w_one)
         columns(p, w_two)

time: 15.4 us -> 15.4 us (level)
  no operation moved by 1% of the time
where the time goes in v8:
time: 15.4 us; the launch traced here: 15.2 us
  Pallas kernels  15.2 us (99%)
    pallas_call x1, Pallas kernels, body(): pl.pallas_call(functools.partial(advance_kernel, rows, panels, voxels, *s...  13 us
    pallas_call x1, Pallas kernels, body(): pl.pallas_call(functools.partial(finish_kernel, rows, panels), out_shape=...  2.22 us

profile of v8, /device:TPU:63, one launch (start us, length us, event | category | flops | bytes accessed | tf_op | source)
XLA Modules:
  0.0 15.2 jit_solution(59755871784261868)
XLA Ops:
  0.0 13.0 %halo_and_columns.1 = (f32[16,512,128]{2,1,0:T(8,128)S(1)}, f32[16,32,128]{2,1,0:T(8,128)S(1)}, f32[16,272,128]{2,1,0:T(8,128)S(1)}, f32[16,272,128]{2,1,0:T(8,1...) custom-call(f32[512,2048]{1,0:T(8,128)} %cov.1, ...), custom_call_target="tpu_custom_call" | custom-call | tf_op jit(solution)/shard_map/halo_and_columns/pallas_call | solution.py:551
  13.0 2.2 %rows.1 = f32[512,2048]{1,0:T(8,128)} custom-call(f32[16,512,128]{2,1,0:T(8,128)S(1)} %get-tuple-element.16.stage, f32[16,32,128]{2,1,0:T(8,128)S(1)} %get-tuple-element.17.u_edge, f32[16,272,128]{2,1,0:T(8,128)S(1)} %get-tuple-element.18.ge, f32[16,272,128]{2,1,0:T(8,128)S(1)} %get-tuple-element.19.go, f32[4,256,128]{2,1,0:T(8,128)S(1)} %get-tuple-element.20.full, ...), custom_call_target="tpu_custom_call" | custom-call | tf_op jit(solution)/shard_map/rows/pallas_call | solution.py:603
